TPU v7x, 32 devices: a whole 2x2x4 slice. The times are simulated.
32 devices in a mesh: dp: 1, seq: 16 (over z, y, x), head: 2 (over core).
Axes of the slice: x: 2, y: 2, z: 4, core: 2. Of those that a mesh axis runs over, the one named last changes fastest.
Arguments:
- query_rows: bfloat16 [1, 4096, 4096], P('dp', 'seq', 'head'), may hold values from -0.59765625 to 0.59765625
- key_rows: bfloat16 [1, 4096, 4096], P('dp', 'seq', 'head'), may hold values from -0.59765625 to 0.59765625
- value_rows: bfloat16 [1, 4096, 4096], P('dp', 'seq', 'head'), may hold values from -1536 to 1536
- grad_out: bfloat16 [1, 4096, 6144], P('dp', 'seq'), may hold values from -6 to 6
- out_weight: bfloat16 [6144, 4096], P('seq', 'head'), may hold values from -0.09375 to 0.09375
- decay_rates: float32 [32], P('head'), may hold values from 0 to 1, as said below
- doc_blocks: int32 [1, 32], P('dp'), may hold values from 0 to 3, never falling along the last dimension, each value on 1 to 16 neighbouring positions
Outputs:
- grad_query: bfloat16 [1, 4096, 4096], P('dp', 'seq', 'head')
- grad_key: bfloat16 [1, 4096, 4096], P('dp', 'seq', 'head')
- grad_value: bfloat16 [1, 4096, 4096], P('dp', 'seq', 'head')
- grad_weight: float32 [6144, 4096], P('seq', 'head')
Inputs may be any that keep to these rules, and one draw needn't show every extreme that they name: `doc_blocks`: in each pack document numbers never fall from block to block; every document covers 1 to 16 blocks, and one covers exactly 16. `decay_rates`: rates are positive.
All inputs are finite; a program needn't handle non-finite values.
Results may differ from a plain program's by a relative error of at most 0.024.
Values may be sent and summed in bfloat16 or wider, within the bound.
A program may use at most 192 MiB of HBM per device.

v0:
```python
import jax
import jax.numpy as jnp
from jax import lax
from jax.sharding import PartitionSpec as P

BLOCK = 128


EPSILON = 1e-05


def prefix(array, axis, join, neutral, backward):
    count = lax.axis_size(axis)
    place = lax.axis_index(axis)
    ahead = count - 1 - place if backward else place
    gathered = jax.tree.map(
        lambda a, kind: lax.all_gather(a.astype(kind), axis), array, (jnp.bfloat16, jnp.bfloat16)
    )
    state = jax.tree.map(lambda a, e: jnp.zeros_like(a) + jnp.asarray(e, a.dtype), array, neutral)

    def one(step, state):
        source = count - 1 - step if backward else step
        return join(
            state,
            jax.tree.map(
                lambda a, own: lax.dynamic_index_in_dim(a, source, 0, False).astype(own.dtype),
                gathered,
                array,
            ),
        )

    return lax.fori_loop(0, ahead, one, state)


def block_docs(doc_row, first_block, block_count, block_len):
    blocks = lax.dynamic_slice_in_dim(doc_row, first_block, block_count)
    return jnp.reshape(
        jnp.broadcast_to(blocks[:, None], (block_count, block_len)), (block_count * block_len,)
    )


def decay_masks(token_docs, decay_rates, prev_doc, next_doc):
    length = token_docs.shape[0]
    position = jnp.arange(length).astype(jnp.float32)
    rates = decay_rates[:, None]
    distance = position[:, None] - position[None, :]
    allowed = jnp.logical_and(distance >= 0, token_docs[:, None] == token_docs[None, :])
    intra = jnp.where(
        allowed[None], jnp.exp(-rates[:, :, None] * jnp.maximum(distance, 0.0)[None]), 0.0
    )
    weight_end = jnp.where(
        (token_docs == token_docs[length - 1])[None],
        jnp.exp(-rates * (length - 1.0 - position)[None]),
        0.0,
    )
    weight_start = jnp.where(
        (token_docs == token_docs[0])[None], jnp.exp(-rates * position[None]), 0.0
    )
    weight_before = jnp.where(
        (token_docs == prev_doc)[None], jnp.exp(-rates * (position + 1.0)[None]), 0.0
    )
    weight_after = jnp.where(
        (token_docs == next_doc)[None], jnp.exp(-rates * (length - position)[None]), 0.0
    )
    span_decay = jnp.exp(-decay_rates * float(length))
    link_fwd = jnp.where(token_docs[length - 1] == prev_doc, span_decay, 0.0)
    link_rev = jnp.where(token_docs[0] == next_doc, span_decay, 0.0)
    return (intra, weight_end, weight_start, weight_before, weight_after, link_fwd, link_rev)


def combine_states(earlier, later):
    return (earlier[0] * later[0], later[0][:, None, None] * earlier[1] + later[1])


def local_state(keys_here, values_here, weight_end):
    weighted = (keys_here.astype(jnp.float32) * weight_end.T[:, :, None]).astype(jnp.bfloat16)
    return jnp.einsum("jhd,jhe->hde", weighted, values_here, preferred_element_type=jnp.float32)


def forward_out(queries, keys_here, values_here, intra, weight_before, state_in):
    scores = jnp.einsum("thd,jhd->htj", queries, keys_here, preferred_element_type=jnp.float32)
    attention = (scores * intra).astype(jnp.bfloat16)
    state_low = state_in.astype(jnp.bfloat16)
    carried = jnp.einsum("thd,hde->the", queries, state_low, preferred_element_type=jnp.float32)
    output = (
        jnp.einsum("htj,jhe->the", attention, values_here, preferred_element_type=jnp.float32)
        + weight_before.T[:, :, None] * carried
    )
    inverse_rms = lax.rsqrt(jnp.mean(output * output, axis=-1, keepdims=True) + EPSILON)
    return (attention, state_low, output * inverse_rms, inverse_rms)


def backward_local(queries, values_here, intra, normal, inverse_rms, grad_normed, weight_start):
    inner = jnp.mean(grad_normed * normal, axis=-1, keepdims=True)
    grad_attn = (inverse_rms * (grad_normed - normal * inner)).astype(jnp.bfloat16)
    grad_scores = (
        jnp.einsum("the,jhe->htj", grad_attn, values_here, preferred_element_type=jnp.float32)
        * intra
    ).astype(jnp.bfloat16)
    weighted = (queries.astype(jnp.float32) * weight_start.T[:, :, None]).astype(jnp.bfloat16)
    back_local = jnp.einsum("thd,the->hde", weighted, grad_attn, preferred_element_type=jnp.float32)
    return (grad_attn, grad_scores, back_local)


def backward_rest(
    queries,
    keys_here,
    values_here,
    attention,
    state_low,
    grad_attn,
    grad_scores,
    weight_before,
    weight_after,
    state_back,
):
    back_low = state_back.astype(jnp.bfloat16)
    grad_query = jnp.einsum(
        "htj,jhd->thd", grad_scores, keys_here, preferred_element_type=jnp.float32
    ) + weight_before.T[:, :, None] * jnp.einsum(
        "the,hde->thd", grad_attn, state_low, preferred_element_type=jnp.float32
    )
    grad_key = jnp.einsum(
        "htj,thd->jhd", grad_scores, queries, preferred_element_type=jnp.float32
    ) + weight_after.T[:, :, None] * jnp.einsum(
        "jhe,hde->jhd", values_here, back_low, preferred_element_type=jnp.float32
    )
    grad_value = jnp.einsum(
        "htj,the->jhe", attention, grad_attn, preferred_element_type=jnp.float32
    ) + weight_after.T[:, :, None] * jnp.einsum(
        "jhd,hde->jhe", keys_here, back_low, preferred_element_type=jnp.float32
    )
    return (
        grad_query.astype(jnp.bfloat16),
        grad_key.astype(jnp.bfloat16),
        grad_value.astype(jnp.bfloat16),
    )


def local(query_rows, key_rows, value_rows, grad_out, out_weight, decay_rates, doc_blocks):
    tok_count = query_rows.shape[1]
    heads_here = decay_rates.shape[0]
    head_dim = query_rows.shape[2] // heads_here
    seq_count = lax.axis_size("seq")
    span_index = lax.axis_index("seq")
    block_count = tok_count // BLOCK
    total_blocks = doc_blocks.shape[1]
    queries = query_rows[0].reshape(tok_count, heads_here, head_dim)
    keys_here = key_rows[0].reshape(tok_count, heads_here, head_dim)
    values_here = value_rows[0].reshape(tok_count, heads_here, head_dim)
    grad_rows = grad_out[0]
    doc_row = doc_blocks[0]
    first_block = span_index * block_count
    token_docs = block_docs(doc_row, first_block, block_count, BLOCK)
    prev_doc = doc_row[jnp.maximum(first_block - 1, 0)]
    next_doc = doc_row[jnp.minimum(first_block + block_count, total_blocks - 1)]
    intra, weight_end, weight_start, weight_before, weight_after, link_fwd, link_rev = decay_masks(
        token_docs, decay_rates, prev_doc, next_doc
    )
    state_local = local_state(keys_here, values_here, weight_end)
    identity = (jnp.ones_like(link_fwd), jnp.zeros_like(state_local))
    state_in = prefix((link_fwd, state_local), "seq", combine_states, identity, False)[1]
    attention, state_low, normal, inverse_rms = forward_out(
        queries, keys_here, values_here, intra, weight_before, state_in
    )
    columns = grad_rows
    grad_normed = jnp.dot(
        columns,
        lax.all_gather(out_weight, "seq", axis=0, tiled=True),
        preferred_element_type=jnp.float32,
    )
    normed = normal.astype(jnp.bfloat16).reshape(tok_count, heads_here * head_dim)
    columns = grad_rows
    part = lax.dot_general(
        columns, normed, (((0,), (0,)), ((), ())), preferred_element_type=jnp.float32
    )
    weight_part = lax.psum_scatter(
        part.astype(jnp.bfloat16).astype(jnp.float32).astype(jnp.bfloat16),
        "seq",
        scatter_dimension=0,
        tiled=True,
    )
    norm_factor = (lax.axis_size("dp") * seq_count * tok_count) ** (-0.5)
    grad_weight = lax.psum(weight_part, "dp").astype(jnp.float32) * norm_factor
    grad_attn, grad_scores, back_local = backward_local(
        queries,
        values_here,
        intra,
        normal,
        inverse_rms,
        grad_normed.reshape(tok_count, heads_here, head_dim),
        weight_start,
    )
    back_identity = (jnp.ones_like(link_rev), jnp.zeros_like(back_local))
    state_back = prefix((link_rev, back_local), "seq", combine_states, back_identity, True)[1]
    grad_query, grad_key, grad_value = backward_rest(
        queries,
        keys_here,
        values_here,
        attention,
        state_low,
        grad_attn,
        grad_scores,
        weight_before,
        weight_after,
        state_back,
    )
    flat_shape = (1, tok_count, heads_here * head_dim)
    return (
        grad_query.reshape(flat_shape),
        grad_key.reshape(flat_shape),
        grad_value.reshape(flat_shape),
        grad_weight,
    )


def solution(mesh):
    in_specs = (
        P("dp", "seq", "head"),
        P("dp", "seq", "head"),
        P("dp", "seq", "head"),
        P("dp", "seq", None),
        P("seq", "head"),
        P("head"),
        P("dp", None),
    )
    out_specs = (
        P("dp", "seq", "head"),
        P("dp", "seq", "head"),
        P("dp", "seq", "head"),
        P("seq", "head"),
    )
    return jax.shard_map(local, mesh=mesh, in_specs=in_specs, out_specs=out_specs, check_vma=False)
```

profile of v0, /device:TPU:0, one launch (start us, length us, event | category | flops | bytes accessed | tf_op | source)
XLA Modules:
  0.0 954.3 jit_solution(3685641747650519546)
XLA Ops:
  12.7 2.7 bitcast_compare_fusion.3
  15.4 2.4 copy.63
  17.8 2.4 copy.36
  26.6 44.2 %all-reduce.2 = (bf16[256]{0:T(256)(128)(2,1)S(1)}, bf16[256]{0:T(256)(128)(2,1)S(1)}) all-reduce(bf16[256]{0:T(256)(128)(2,1)S(1)} %dynamic-update-slice, bf16[256]{0:T(256)(128)(2,1)S(1)} %dynamic-update-slice.1), channel_id=2, replica_groups=mesh['dp'=1,'seq'=16,'head'=2] {'seq'}, use_global_device_ids=true, to_apply=%add | all-reduce | flops 512 | bytes 2048
  70.9 2.3 copy.62
  73.4 2.9 multiply_convert_fusion.1
  77.7 2.2 fusion.14
  79.9 60.2 %all-gather.10.cloned.1.call-done = bf16[256,128,128]{2,1,0:T(8,128)(2,1)} async-done(((bf16[16,128,128]{2,1,0:T(8,128)(2,1)}), bf16[256,128,128]{2,1,0:T(8,128)(2,1)}) %all-gather.10.cloned.1.call-update) | async-done | bytes 8388624 | tf_op jit(solution)/shard_map/all_gather | solution.py:17
  141.1 4.1 multiply_reduce_fusion.1
  145.3 267.0 %all-gather.8.cloned.1.call-done = bf16[6144,2048]{1,0:T(8,128)(2,1)} async-done(((bf16[384,2048]{1,0:T(8,128)(2,1)}), bf16[6144,2048]{1,0:T(8,128)(2,1)}) %all-gather.8.cloned.1.call-update) | async-done | bytes 25165840 | tf_op jit(solution)/shard_map/all_gather | solution.py:169
  412.3 32.3 %copy.40 = bf16[2048,6144]{1,0:T(8,128)(2,1)} copy(bf16[2048,6144]{0,1:T(8,128)(2,1)} %bitcast.103) | data formatting | bytes 50331648 | tf_op jit(solution)/shard_map/dot_general | solution.py:167
  444.6 13.3 %multiply_reduce_fusion = (f32[256,16]{0,1:T(8,128)S(1)}, f32[256,16,128]{0,2,1:T(8,128)S(1)}) fusion(f32[256,16,128]{0,2,1:T(8,128)} %get-tuple-element.182, f32[256,16]{0,1:T(8,128)S(1)} %add_rsqrt_fusion, bf16[16,128,6144]{2,1,0:T(8,128)(2,1)} %bitcast.104, bf16[1,256,6144]{2,1,0:T(8,128)(2,1)S(1)} %copy-done), kind=kOutput, calls=%fused_computation.25 | convolution fusion | flops 6444019712 | bytes 32538624 | tf_op jit(solution)/shard_map/dot_general | solution.py:167
  462.0 13.2 %convert_bitcast_fusion = bf16[6144,2048]{0,1:T(8,128)(2,1)} fusion(bf16[256,2048]{0,1:T(8,128)(2,1)} %bitcast.116, bf16[1,256,6144]{2,1,0:T(8,128)(2,1)S(1)} %copy-done), kind=kOutput, calls=%fused_computation.4 | convolution fusion | flops 6455033856 | bytes 29360128 | tf_op jit(solution)/shard_map/dot_general | solution.py:174
  475.2 32.9 %copy.60 = bf16[6144,2048]{1,0:T(8,128)(2,1)} copy(bf16[6144,2048]{0,1:T(8,128)(2,1)} %convert_bitcast_fusion) | data formatting | bytes 50331648
  514.4 2.3 copy.51
  516.6 3.6 fusion.32
  522.0 50.9 %all-gather.12.cloned.1.call-done = bf16[256,128,128]{2,1,0:T(8,128)(2,1)} async-done(((bf16[16,128,128]{2,1,0:T(8,128)(2,1)}), bf16[256,128,128]{2,1,0:T(8,128)(2,1)}) %all-gather.12.cloned.1.call-update) | async-done | bytes 8388624 | tf_op jit(solution)/shard_map/all_gather | solution.py:17
  573.0 20.4 %while.27 = (s32[]{:T(128)}, f32[16,128,128]{2,1,0:T(8,128)S(1)}, s32[]{:T(128)}, bf16[16,16]{1,0:T(8,128)(2,1)S(1)}, bf16[16,16,128,128]{3,2,1,0:T(8,128)(2,1)}...) while((s32[]{:T(128)}, f32[16,128,128]{2,1,0:T(8,128)S(1)}, s32[]{:T(128)}, bf16[16,16]{1,0:T(8,128)(2,1)S(1)}, ...), condition=%wide.region_5.6_spmd, body=%wide.region_4.5_spmd.sunk | while | flops 786454 | bytes 2621755 | solution.py:32
  593.4 3.1 fusion.4
  596.5 2.3 copy.53
  602.3 335.9 %reduce-scatter.4.cloned.1.call-done = bf16[384,2048]{1,0:T(8,128)(2,1)} async-done(((bf16[6144,2048]{1,0:T(8,128)(2,1)}), bf16[384,2048]{1,0:T(8,128)(2,1)}) %reduce-scatter.4.cloned.1.call-update) | async-done | bytes 1572880
  938.3 2.6 copy.61
  940.8 3.4 convert_multiply_fusion
  944.2 3.5 copy.54
  (109 shorter events, 47.0 us)
Async XLA Ops:
  7.2 437.4 %copy-start = (bf16[1,256,6144]{2,1,0:T(8,128)(2,1)S(1)}, bf16[1,256,6144]{2,1,0:T(8,128)(2,1)}, u32[]{:S(2)}) copy-start(bf16[1,256,6144]{2,1,0:T(8,128)(2,1)} %param.14) | copy-start | bytes 9437188
  7.2 132.9 %all-gather.10.cloned.1.call-start = ((), (), s32[]{:S(2)}) async-start(), calls=%async_computation.2 | async-start | bytes 8912896 | tf_op jit(solution)/shard_map/all_gather | solution.py:17
  17.8 4.0 copy-start.17
  20.2 2.5 copy-start.15
  21.8 1.0 copy-start.7
  22.7 2.1 copy-start.18
  24.1 388.2 %all-gather.8.cloned.1.call-start = ((), (), s32[]{:S(2)}) async-start(), calls=%async_computation.1 | async-start | bytes 26738688 | tf_op jit(solution)/shard_map/all_gather | solution.py:169
  24.8 548.1 %all-gather.12.cloned.1.call-start = ((), (), s32[]{:S(2)}) async-start(), calls=%async_computation.3 | async-start | bytes 8912896 | tf_op jit(solution)/shard_map/all_gather | solution.py:17
  73.4 4.3 copy-start.8
  76.4 1.4 copy-start.12
  444.6 13.3 %copy-start.11 = (f32[256,16,128]{0,2,1:T(8,128)S(1)}, f32[256,16,128]{0,2,1:T(8,128)}, u32[]{:S(2)}) copy-start(f32[256,16,128]{0,2,1:T(8,128)} %get-tuple-element.182) | copy-start | bytes 6291460
  457.9 2.6 copy-start.5
  459.5 1.0 copy-start.3
  461.7 476.5 %reduce-scatter.4.cloned.1.call-start = ((), (), s32[]{:S(2)}) async-start(), calls=%async_computation.4 | async-start | bytes 26738688
  508.1 1.2 copy-start.4
  508.1 1.5 copy-start.9
  509.6 1.3 copy-start.16
  510.9 1.3 copy-start.13
  510.9 2.0 copy-start.2
  516.6 3.6 copy-start.6
  516.6 3.6 copy-start.14
  573.0 20.4 %copy-start.10 = (bf16[32,8,16,128]{3,2,1,0:T(8,128)(2,1)S(1)}, bf16[32,8,16,128]{3,2,1,0:T(8,128)(2,1)}, u32[]{:S(2)}) copy-start(bf16[32,8,16,128]{3,2,1,0:T(8,128)(2,1)} %copy.63) | copy-start | bytes 3145732
  940.8 6.9 copy-start.1
Sparse Core Ops, SparseCore 0:
  24.2 115.8 all-gather.9
  142.8 269.4 all-gather.7
  461.9 111.0 all-gather.11
  578.5 359.7 reduce-scatter.3
where the time goes:
time: 957 us; the launch traced here: 954 us
  waiting for transfers between devices  715 us (75%)
  local copies, waits for them, and re-layouts  97 us (10%)
  matrix products  52.3 us (5%)
  blocking collectives  44.2 us (5%)
  other arithmetic  27.9 us (3%)
  between operations  17.3 us (2%)
    unnamed x5, waiting for transfers between devices  337 us
    all_gather x1, waiting for transfers between devices, local(): lax.all_gather(out_weight, 'seq', axis=0, tiled=True)  267 us
    all_gather x2, waiting for transfers between devices, prefix(): lax.all_gather(a.astype(kind), axis)  111 us
    unnamed x51, local copies, waits for them, and re-layouts  55.8 us
    unnamed x1, blocking collectives  44.2 us
    dot_general x1, local copies, waits for them, and re-layouts, local(): jnp.dot(columns, lax.all_gather(out_weight, 'seq', axis=0, tiled=True), p...  32.3 us
    add x15, other arithmetic, combine_states(): later[0][:, None, None] * earlier[1] + later[1]  19.7 us
  transfers between devices with their start and end apart: 4, of which 4 were waited for; matrix products, arithmetic and copies ran while one was open for 10% of the time, Pallas kernels for 0%

commit v1 on v0

v1 whole, which is shorter than its diff:
```python
import functools

import jax
import jax.numpy as jnp
from jax import lax
from jax.experimental import pallas as pl
from jax.experimental.pallas import tpu as pltpu
from jax.sharding import Mesh, PartitionSpec as P

BLOCK = 128
EPSILON = 1e-05
SEQ = ("sa", "sb")
F32 = jnp.float32
BF16 = jnp.bfloat16


def mm(a, b, ca, cb):
    return lax.dot_general(a, b, (((ca,), (cb,)), ((), ())), preferred_element_type=F32)


def column(mask_ref, index, rate, offset, sign):
    length = mask_ref.shape[0]
    position = lax.broadcasted_iota(jnp.int32, (length, 1), 0).astype(F32)
    return mask_ref[:, index : index + 1] * jnp.exp(-rate * (offset + sign * position))


def intra_of(allowed_ref, rate):
    shape = allowed_ref.shape
    distance = lax.broadcasted_iota(jnp.int32, shape, 0) - lax.broadcasted_iota(jnp.int32, shape, 1)
    return allowed_ref[...] * jnp.exp(-rate * jnp.maximum(distance, 0).astype(F32))


def attend(rate, allowed_ref, mask_ref, q, k, v, state):
    intra = intra_of(allowed_ref, rate)
    attention = (mm(q, k, 1, 1) * intra).astype(BF16)
    before = column(mask_ref, 2, rate, 1.0, 1.0)
    out = mm(attention, v, 1, 0) + before * mm(q, state, 1, 0)
    inverse_rms = lax.rsqrt(jnp.mean(out * out, axis=-1, keepdims=True) + EPSILON)
    return intra, attention, before, out * inverse_rms, inverse_rms


def local_state_kernel(rates, masks, k_ref, v_ref, out_ref):
    rate = rates[pl.program_id(0)]
    end = column(masks, 0, rate, masks.shape[0] - 1.0, -1.0)
    weighted = (k_ref[...].astype(F32) * end).astype(BF16)
    out_ref[0] = mm(weighted, v_ref[...], 0, 0).astype(BF16)


def forward_kernel(rates, masks, allowed, q, k, v, state, out_ref):
    rate = rates[pl.program_id(0)]
    normal = attend(rate, allowed, masks, q[...], k[...], v[...], state[0])[3]
    out_ref[...] = normal.astype(BF16)


def back_state_kernel(rates, masks, allowed, q, k, v, state, gn, grad_ref, out_ref):
    rate = rates[pl.program_id(0)]
    _, _, _, normal, inverse_rms = attend(
        rate, allowed, masks, q[...], k[...], v[...], state[0]
    )
    grad_normed = gn[...].astype(F32)
    inner = jnp.mean(grad_normed * normal, axis=-1, keepdims=True)
    grad = (inverse_rms * (grad_normed - normal * inner)).astype(BF16)
    grad_ref[...] = grad
    start = column(masks, 1, rate, 0.0, 1.0)
    weighted = (q[...].astype(F32) * start).astype(BF16)
    out_ref[0] = mm(weighted, grad, 0, 0).astype(BF16)


def grads_kernel(rates, masks, allowed, q, k, v, state, back, grad, gq_ref, gk_ref, gv_ref):
    rate = rates[pl.program_id(0)]
    intra = intra_of(allowed, rate)
    attention = (mm(q[...], k[...], 1, 1) * intra).astype(BF16)
    before = column(masks, 2, rate, 1.0, 1.0)
    after = column(masks, 3, rate, masks.shape[0] * 1.0, -1.0)
    scores = (mm(grad[...], v[...], 1, 1) * intra).astype(BF16)
    gq = mm(scores, k[...], 1, 0) + before * mm(grad[...], state[0], 1, 1)
    gk = mm(scores, q[...], 0, 0) + after * mm(v[...], back[0], 1, 1)
    gv = mm(attention, grad[...], 0, 0) + after * mm(k[...], back[0], 1, 0)
    gq_ref[...] = gq.astype(BF16)
    gk_ref[...] = gk.astype(BF16)
    gv_ref[...] = gv.astype(BF16)


def scan_kernel(backward, link, x_ref, out_ref):
    count = x_ref.shape[0]
    state = jnp.zeros(x_ref.shape[1:], F32)
    for step in range(count):
        s = count - 1 - step if backward else step
        out_ref[s] = state.astype(BF16)
        state = link[s] * state + x_ref[s].astype(F32)


def per_head(kernel, heads, tok, dim, fixed, rows, states, extra_rows, outs, flops):
    smem = pl.BlockSpec(memory_space=pltpu.SMEM)
    row_spec = pl.BlockSpec((tok, dim), lambda h: (0, h))
    state_spec = pl.BlockSpec((1, dim, dim), lambda h: (h, 0, 0))
    in_specs = [smem] + [pl.BlockSpec(a.shape, lambda h: (0, 0)) for a in fixed[1:]]
    in_specs += [row_spec] * len(rows) + [state_spec] * len(states) + [row_spec] * len(extra_rows)
    kinds = {
        "row": (row_spec, jax.ShapeDtypeStruct((tok, heads * dim), BF16)),
        "state": (state_spec, jax.ShapeDtypeStruct((heads, dim, dim), BF16)),
    }
    return pl.pallas_call(
        kernel,
        grid=(heads,),
        in_specs=in_specs,
        out_specs=[kinds[o][0] for o in outs],
        out_shape=[kinds[o][1] for o in outs],
        compiler_params=pltpu.CompilerParams(vmem_limit_bytes=24 * 1024 * 1024),
        cost_estimate=pl.CostEstimate(
            flops=flops * heads,
            bytes_accessed=2 * tok * heads * dim * (len(rows) + len(extra_rows) + len(outs)),
            transcendentals=heads * tok * tok,
        ),
    )(*fixed, *rows, *states, *extra_rows)


def local(query_rows, key_rows, value_rows, grad_out, out_weight, decay_rates, doc_blocks):
    tok = query_rows.shape[1]
    heads = decay_rates.shape[0]
    dim = query_rows.shape[2] // heads
    count = lax.axis_size(SEQ)
    span = lax.axis_index(SEQ)
    blocks = tok // BLOCK
    total = doc_blocks.shape[1]
    docs = doc_blocks[0]
    q, k, v = query_rows[0], key_rows[0], value_rows[0]
    rates = decay_rates

    with jax.named_scope("masks"):
        first = span * blocks
        token_docs = jnp.repeat(lax.dynamic_slice_in_dim(docs, first, blocks), BLOCK)
        prev_doc = docs[jnp.maximum(first - 1, 0)]
        next_doc = docs[jnp.minimum(first + blocks, total - 1)]
        position = jnp.arange(tok)
        allowed = (
            (position[:, None] >= position[None, :]) & (token_docs[:, None] == token_docs[None, :])
        ).astype(F32)
        masks = jnp.stack(
            [
                token_docs == token_docs[tok - 1],
                token_docs == token_docs[0],
                token_docs == prev_doc,
                token_docs == next_doc,
            ],
            axis=1,
        ).astype(F32)
        firsts = jnp.arange(count) * blocks
        join_fwd = docs[firsts + blocks - 1] == docs[jnp.maximum(firsts - 1, 0)]
        join_rev = docs[firsts] == docs[jnp.minimum(firsts + blocks, total - 1)]

    fixed = (rates, masks, allowed)
    one = 2 * tok * dim * dim
    pair = 2 * tok * tok * dim

    with jax.named_scope("grad_columns"):
        halves = lax.axis_size("head")
        part_rows = tok // halves
        mine = lax.dynamic_slice_in_dim(grad_out[0], lax.axis_index("head") * part_rows, part_rows)
        groups = lax.axis_size("sa")
        width = mine.shape[1] // groups
        mine = mine.reshape(part_rows, groups, width).transpose(1, 0, 2)
        mine = lax.all_to_all(mine, "sa", 0, 0, tiled=True)
        columns = lax.all_gather(mine, "head", axis=0)
        columns = columns.transpose(1, 0, 2, 3).reshape(groups * tok, width)
    with jax.named_scope("weight_rows"):
        weight = lax.all_gather(out_weight, "sb", axis=0, tiled=True)

    def weights(join, rate):
        return jnp.where(join, jnp.exp(-rate * float(tok)), 0.0)

    def exchanged(states, join, backward):
        rows = heads * dim // count
        assert dim % rows == 0
        parts = lax.all_to_all(states.reshape(count, rows, dim), SEQ, 0, 0, tiled=True)
        done = pl.pallas_call(
            functools.partial(scan_kernel, backward),
            in_specs=[
                pl.BlockSpec(memory_space=pltpu.SMEM),
                pl.BlockSpec(memory_space=pltpu.VMEM),
            ],
            out_specs=pl.BlockSpec(memory_space=pltpu.VMEM),
            out_shape=jax.ShapeDtypeStruct(parts.shape, BF16),
        )(weights(join, rates[span * rows // dim]), parts)
        return lax.all_to_all(done, SEQ, 0, 0, tiled=True).reshape(heads, dim, dim)

    with jax.named_scope("states"):
        (local_states,) = per_head(
            local_state_kernel, heads, tok, dim, fixed[:2], (k, v), (), (), ("state",), one
        )
        state_low = exchanged(local_states, join_fwd, False)
    with jax.named_scope("forward"):
        (normed,) = per_head(
            forward_kernel, heads, tok, dim, fixed, (q, k, v), (state_low,), (), ("row",),
            2 * pair + one,
        )
    with jax.named_scope("grad_normed"):
        partial = jnp.dot(columns, weight, preferred_element_type=F32).astype(BF16)
        grad_normed = lax.psum_scatter(partial, "sa", scatter_dimension=0, tiled=True)
    with jax.named_scope("grad_weight"):
        normed_group = lax.all_gather(normed, "sa", axis=0, tiled=True)
        part = mm(columns, normed_group, 0, 0).astype(BF16)
        weight_part = lax.psum_scatter(part, "sb", scatter_dimension=0, tiled=True)
        norm_factor = (lax.axis_size("dp") * count * tok) ** (-0.5)
        grad_weight = lax.psum(weight_part, "dp").astype(F32) * norm_factor
    with jax.named_scope("back_states"):
        grad_attn, back_local = per_head(
            back_state_kernel, heads, tok, dim, fixed, (q, k, v), (state_low,), (grad_normed,),
            ("row", "state"), 2 * pair + 2 * one,
        )
        back_low = exchanged(back_local, join_rev, True)
    with jax.named_scope("grads"):
        grads = per_head(
            grads_kernel, heads, tok, dim, fixed, (q, k, v), (state_low, back_low), (grad_attn,),
            ("row", "row", "row"), 5 * pair + 3 * one,
        )
    return (grads[0][None], grads[1][None], grads[2][None], grad_weight)


def solution(mesh):
    dp, seq, head = (mesh.shape[name] for name in ("dp", "seq", "head"))
    outer = 4 if seq % 4 == 0 else 1
    fine = Mesh(mesh.devices.reshape(dp, outer, seq // outer, head), ("dp", "sa", "sb", "head"))
    rows = P("dp", SEQ, "head")
    in_specs = (rows, rows, rows, P("dp", SEQ, None), P(SEQ, "head"), P("head"), P("dp", None))
    out_specs = (rows, rows, rows, P(SEQ, "head"))
    return jax.shard_map(local, mesh=fine, in_specs=in_specs, out_specs=out_specs, check_vma=False)
```

time: 957 us -> 410 us (0.43)
  waiting for transfers between devices: 715 us -> 199 us
  local copies, waits for them, and re-layouts: 97 us -> 38 us
  Pallas kernels: 0 us -> 45.5 us
  matrix products: 52.3 us -> 22.3 us
  other arithmetic: 27.9 us -> 9.16 us
  blocking collectives: 44.2 us -> 61.7 us
  starting transfers between devices: 0.34 us -> 15.3 us
    unnamed x5, waiting for transfers between devices: 337 us -> 0.76 us
    all_gather x3, waiting for transfers between devices: 378 us -> 90.1 us  [the longest x1 71.8 us: local(): normed_group = lax.all_gather(normed, 'sa', axis=0, tiled=True)]
    reduce_scatter x0 -> x2, waiting for transfers between devices: none -> 71.9 us  [the longest x1 66.1 us: local(): lax.psum_scatter(partial, 'sa', scatter_dimension=0, tiled=True)]
    all_to_all x0 -> x2, blocking collectives: none -> 61.7 us  [the longest x1 43.4 us: local(): mine = lax.all_to_all(mine, 'sa', 0, 0, tiled=True)]
    pallas_call x0 -> x6, Pallas kernels: none -> 45.5 us  [the longest x4 41.6 us: per_head(): pl.pallas_call(kernel, grid=(heads,), in_specs=in_specs, out_specs=[kinds...]
    unnamed x1 -> x0, blocking collectives: 44.2 us -> none
    all_to_all x0 -> x3, waiting for transfers between devices: none -> 36.5 us  [the longest x2 22.6 us: exchanged(): lax.all_to_all(states.reshape(count, rows, dim), SEQ, 0, 0, tiled=True)]
    dot_general x1 -> x0, local copies, waits for them, and re-layouts: 32.3 us -> none  [local(): jnp.dot(columns, lax.all_gather(out_weight, 'seq', axis=0, tiled=True), p...]
  transfers between devices with their start and end apart: 4 -> 8, of which waited for: 4 -> 7; matrix products, arithmetic and copies ran while one was open for 10% -> 9% of each run, Pallas kernels for 0% -> 11%
where the time goes in v1:
time: 410 us; the launch traced here: 406 us
  waiting for transfers between devices  199 us (49%)
  blocking collectives  61.7 us (15%)
  Pallas kernels  45.5 us (11%)
  local copies, waits for them, and re-layouts  38 us (9%)
  matrix products  22.3 us (5%)
  starting transfers between devices  15.3 us (4%)
  between operations  14.7 us (4%)
  other arithmetic  9.16 us (2%)
    all_gather x1, waiting for transfers between devices, local(): normed_group = lax.all_gather(normed, 'sa', axis=0, tiled=True)  71.8 us
    reduce_scatter x1, waiting for transfers between devices, local(): lax.psum_scatter(partial, 'sa', scatter_dimension=0, tiled=True)  66.1 us
    all_to_all x1, blocking collectives, local(): mine = lax.all_to_all(mine, 'sa', 0, 0, tiled=True)  43.4 us
    pallas_call x4, Pallas kernels, per_head(): pl.pallas_call(kernel, grid=(heads,), in_specs=in_specs, out_specs=[kinds...  41.6 us
    unnamed x46, local copies, waits for them, and re-layouts  25.2 us
    all_to_all x2, waiting for transfers between devices, exchanged(): lax.all_to_all(states.reshape(count, rows, dim), SEQ, 0, 0, tiled=True)  22.6 us
    all_to_all x1, blocking collectives, exchanged(): return lax.all_to_all(done, SEQ, 0, 0, tiled=True).reshape(heads, dim, dim)  18.3 us
    all_gather x1, waiting for transfers between devices, local(): weight = lax.all_gather(out_weight, 'sb', axis=0, tiled=True)  18.3 us
  transfers between devices with their start and end apart: 8, of which 7 were waited for; matrix products, arithmetic and copies ran while one was open for 9% of the time, Pallas kernels for 11%

profile of v1, /device:TPU:0, one launch (start us, length us, event | category | flops | bytes accessed | tf_op | source)
XLA Modules:
  0.0 406.0 jit_solution(11490661472483821745)
XLA Ops:
  10.3 2.6 copy.31
  12.9 43.4 %all_to_all.25 = bf16[4,128,1536]{1,2,0:T(8,128)(2,1)} all-to-all(bf16[4,128,1536]{1,2,0:T(8,128)(2,1)} %bitcast.77), channel_id=1, replica_groups=mesh['dp'=1,'sa'=4,'sb'=4,'head'=2] {'sa'}, dimensions={0} | all-to-all | bytes 3145728 | tf_op jit(solution)/shard_map/grad_columns/all_to_all | solution.py:163
  56.3 2.6 copy.29
  66.8 6.1 %states.2 = bf16[16,128,128]{2,1,0:T(8,128)(2,1)S(1)} custom-call(f32[16]{0:T(128)S(1)} %copy-done.16, f32[256,4]{1,0:T(8,128)S(1)} %convert_element_type.15.masks, bf16[256,2048]{1,0:T(8,128)(2,1)S(1)} %bitcast.62, bf16[256,2048]{1,0:T(8,128)(2,1)S(1)} %bitcast.66), custom_call_target="tpu_custom_call" | custom-call | flops 134217728 | bytes 3145728 | tf_op jit(solution)/shard_map/states/pallas_call | solution.py:103
  73.7 4.6 %all-to-all-start = ((bf16[16,128,128]{2,1,0:T(8,128)(2,1)}), bf16[16,128,128]{2,1,0:T(8,128)(2,1)}, u32[]{:S(2)}, u32[]{:S(2)}) async-start(bf16[16,128,128]{2,1,0:T(8,128)(2,1)} %copy-done.13), calls=%async_computation | async-start | bytes 1048576 | tf_op jit(solution)/shard_map/states/all_to_all | solution.py:175
  82.0 11.0 %all-to-all-done.x_ref = bf16[16,128,128]{2,1,0:T(8,128)(2,1)} async-done(((bf16[16,128,128]{2,1,0:T(8,128)(2,1)}), bf16[16,128,128]{2,1,0:T(8,128)(2,1)}, u32[]{:S(2)}, u32[]{:S(2)}) %all-to-all-start) | async-done | bytes 524320 | tf_op jit(solution)/shard_map/states/all_to_all | solution.py:175
  93.0 2.0 states.3
  95.0 4.2 %all-to-all-start.1 = ((bf16[16,128,128]{2,1,0:T(8,128)(2,1)}), bf16[16,128,128]{2,1,0:T(8,128)(2,1)}, u32[]{:S(2)}, u32[]{:S(2)}) async-start(bf16[16,128,128]{2,1,0:T(8,128)(2,1)} %states.3), calls=%async_computation.1 | async-start | bytes 1048576 | tf_op jit(solution)/shard_map/states/all_to_all | solution.py:185
  99.4 13.9 %all-to-all-done.1.state = bf16[16,128,128]{2,1,0:T(8,128)(2,1)} async-done(((bf16[16,128,128]{2,1,0:T(8,128)(2,1)}), bf16[16,128,128]{2,1,0:T(8,128)(2,1)}, u32[]{:S(2)}, u32[]{:S(2)}) %all-to-all-start.1) | async-done | bytes 524320 | tf_op jit(solution)/shard_map/states/all_to_all | solution.py:185
  117.5 10.7 %forward.1 = bf16[256,2048]{1,0:T(8,128)(2,1)S(1)} custom-call(f32[16]{0:T(128)S(1)} %copy-done.16, f32[256,4]{1,0:T(8,128)S(1)} %convert_element_type.15.masks, f32[256,256]{1,0:T(8,128)S(1)} %fusion.1.allowed, bf16[256,2048]{1,0:T(8,128)(2,1)S(1)} %bitcast.70, bf16[256,2048]{1,0:T(8,128)(2,1)S(1)} %bitcast.63, bf16[256,2048]{1,0:T(8,128)(2,1)S(1)} %bitcast.67, ...), custom_call_target="tpu_custom_call" | custom-call | flops 671088640 | bytes 4194304 | tf_op jit(solution)/shard_map/forward/pallas_call | solution.py:103
  129.3 3.8 copy.30
  133.0 18.3 %all-gather.5.cloned.1.call-done = bf16[1536,2048]{1,0:T(8,128)(2,1)} async-done(((bf16[384,2048]{1,0:T(8,128)(2,1)}), bf16[1536,2048]{1,0:T(8,128)(2,1)}) %all-gather.5.cloned.1.call-update) | async-done | bytes 6291472 | tf_op jit(solution)/shard_map/weight_rows/all_gather | solution.py:167
  151.3 11.0 %convolution_convert_fusion.1 = bf16[1024,2048]{1,0:T(8,128)(2,1)} fusion(bf16[1024,1536]{1,0:T(8,128)(2,1)} %bitcast.79, bf16[1536,2048]{1,0:T(8,128)(2,1)} %all-gather.5.cloned.1.call-done), kind=kOutput, calls=%fused_computation.5 | convolution fusion | flops 6444548096 | bytes 13631488 | tf_op jit(solution)/shard_map/grad_normed/dot_general | solution.py:198
  162.4 71.8 %all-gather.7.cloned.1.call-done = bf16[1024,2048]{1,0:T(8,128)(2,1)} async-done(((bf16[256,2048]{1,0:T(8,128)(2,1)}), bf16[1024,2048]{1,0:T(8,128)(2,1)}) %all-gather.7.cloned.1.call-update) | async-done | bytes 4194320 | tf_op jit(solution)/shard_map/grad_weight/all_gather | solution.py:201
  234.2 11.3 %convolution_convert_fusion = bf16[1536,2048]{1,0:T(8,128)(2,1)} fusion(bf16[1024,1536]{1,0:T(8,128)(2,1)} %bitcast.80, bf16[1024,2048]{1,0:T(8,128)(2,1)} %all-gather.7.cloned.1.call-done), kind=kOutput, calls=%fused_computation.4 | convolution fusion | flops 6445596672 | bytes 13631488 | tf_op jit(solution)/shard_map/grad_weight/dot_general | solution.py:18
  245.6 66.1 %reduce-scatter.3.cloned.1.call-done.gn = bf16[256,2048]{1,0:T(8,128)(2,1)} async-done(((bf16[1024,2048]{1,0:T(8,128)(2,1)}), bf16[256,2048]{1,0:T(8,128)(2,1)}) %reduce-scatter.3.cloned.1.call-update) | async-done | bytes 1048592 | tf_op jit(solution)/shard_map/grad_normed/reduce_scatter | solution.py:199
  316.6 12.9 %back_states.2 = (bf16[256,2048]{1,0:T(8,128)(2,1)S(1)}, bf16[16,128,128]{2,1,0:T(8,128)(2,1)S(1)}) custom-call(f32[16]{0:T(128)S(1)} %copy-done.16, f32[256,4]{1,0:T(8,128)S(1)} %convert_element_type.15.masks, f32[256,256]{1,0:T(8,128)S(1)} %fusion.1.allowed, bf16[256,2048]{1,0:T(8,128)(2,1)S(1)} %bitcast.71, bf16[256,2048]{1,0:T(8,128)(2,1)S(1)} %bitcast.64, ...), custom_call_target="tpu_custom_call" | custom-call | flops 805306368 | bytes 6291456 | tf_op jit(solution)/shard_map/back_states/pallas_call | solution.py:103
  331.3 6.2 %all-to-all-start.3 = ((bf16[16,128,128]{2,1,0:T(8,128)(2,1)}), bf16[16,128,128]{2,1,0:T(8,128)(2,1)}, u32[]{:S(2)}, u32[]{:S(2)}) async-start(bf16[16,128,128]{2,1,0:T(8,128)(2,1)} %copy-done.15), calls=%async_computation.4 | async-start | bytes 1048576 | tf_op jit(solution)/shard_map/back_states/all_to_all | solution.py:175
  341.2 11.6 %all-to-all-done.3.x_ref = bf16[16,128,128]{2,1,0:T(8,128)(2,1)} async-done(((bf16[16,128,128]{2,1,0:T(8,128)(2,1)}), bf16[16,128,128]{2,1,0:T(8,128)(2,1)}, u32[]{:S(2)}, u32[]{:S(2)}) %all-to-all-start.3) | async-done | bytes 524320 | tf_op jit(solution)/shard_map/back_states/all_to_all | solution.py:175
  352.7 2.0 back_states.3
  354.7 18.3 %all_to_all.26.back = bf16[16,128,128]{2,1,0:T(8,128)(2,1)S(1)} all-to-all(bf16[16,128,128]{2,1,0:T(8,128)(2,1)} %back_states.3), channel_id=1, replica_groups=mesh['dp'=1,'sa'=4,'sb'=4,'head'=2] {'sa','sb'}, dimensions={0} | all-to-all | bytes 1048576 | tf_op jit(solution)/shard_map/back_states/all_to_all | solution.py:185
  378.2 12.0 %grads.1 = (bf16[256,2048]{1,0:T(8,128)(2,1)}, bf16[256,2048]{1,0:T(8,128)(2,1)}, bf16[256,2048]{1,0:T(8,128)(2,1)}) custom-call(f32[16]{0:T(128)S(1)} %copy-done.16, f32[256,4]{1,0:T(8,128)S(1)} %convert_element_type.15.masks, f32[256,256]{1,0:T(8,128)S(1)} %fusion.1.allowed, bf16[256,2048]{1,0:T(8,128)(2,1)S(1)} %bitcast.72, ...), custom_call_target="tpu_custom_call" | custom-call | flops 1744830464 | bytes 7340032 | tf_op jit(solution)/shard_map/grads/pallas_call | solution.py:103
  390.2 5.8 %reduce-scatter.5.cloned.1.call-done = bf16[384,2048]{1,0:T(8,128)(2,1)} async-done(((bf16[1536,2048]{1,0:T(8,128)(2,1)}), bf16[384,2048]{1,0:T(8,128)(2,1)}) %reduce-scatter.5.cloned.1.call-update) | async-done | bytes 1572880 | tf_op jit(solution)/shard_map/grad_weight/reduce_scatter | solution.py:203
  396.0 3.5 convert_multiply_fusion
  (80 shorter events, 35.7 us)
Async XLA Ops:
  7.2 1.9 copy-start
  7.2 122.1 %all-gather.9.cloned.1.call-start = ((), (), s32[]{:S(2)}) async-start(), calls=%async_computation.11 | async-start | bytes 4718592 | tf_op jit(solution)/shard_map/grad_columns/all_gather | solution.py:164
  56.3 3.4 copy-start.19
  56.3 7.8 %copy-start.16 = (f32[16]{0:T(128)S(1)}, f32[16]{0:T(128)}, u32[]{:S(2)}) copy-start(f32[16]{0:T(128)} %rates.7) | copy-start | bytes 196
  58.9 92.4 %all-gather.5.cloned.1.call-start = ((), (), s32[]{:S(2)}) async-start(), calls=%async_computation.7 | async-start | bytes 7864320 | tf_op jit(solution)/shard_map/weight_rows/all_gather | solution.py:167
  64.1 1.3 copy-start.1
  65.4 1.4 copy-start.5
  73.7 19.3 %all-to-all-start = ((bf16[16,128,128]{2,1,0:T(8,128)(2,1)}), bf16[16,128,128]{2,1,0:T(8,128)(2,1)}, u32[]{:S(2)}, u32[]{:S(2)}) async-start(bf16[16,128,128]{2,1,0:T(8,128)(2,1)} %copy-done.13), calls=%async_computation | async-start | bytes 1048576 | tf_op jit(solution)/shard_map/states/all_to_all | solution.py:175
  95.0 18.3 %all-to-all-start.1 = ((bf16[16,128,128]{2,1,0:T(8,128)(2,1)}), bf16[16,128,128]{2,1,0:T(8,128)(2,1)}, u32[]{:S(2)}, u32[]{:S(2)}) async-start(bf16[16,128,128]{2,1,0:T(8,128)(2,1)} %states.3), calls=%async_computation.1 | async-start | bytes 1048576 | tf_op jit(solution)/shard_map/states/all_to_all | solution.py:185
  99.2 135.0 %all-gather.7.cloned.1.call-start = ((), (), s32[]{:S(2)}) async-start(), calls=%async_computation.9 | async-start | bytes 5242880 | tf_op jit(solution)/shard_map/grad_weight/all_gather | solution.py:201
  113.3 1.2 copy-start.2
  114.5 1.5 copy-start.6
  116.0 1.5 copy-start.10
  129.2 182.5 %reduce-scatter.3.cloned.1.call-start = ((), (), s32[]{:S(2)}) async-start(), calls=%async_computation.8 | async-start | bytes 5242880 | tf_op jit(solution)/shard_map/grad_normed/reduce_scatter | solution.py:199
  162.4 233.7 %reduce-scatter.5.cloned.1.call-start = ((), (), s32[]{:S(2)}) async-start(), calls=%async_computation.10 | async-start | bytes 7864320 | tf_op jit(solution)/shard_map/grad_weight/reduce_scatter | solution.py:203
  311.7 1.2 copy-start.3
  312.9 1.2 copy-start.7
  314.2 1.2 copy-start.11
  315.4 1.2 copy-start.14
  331.3 21.4 %all-to-all-start.3 = ((bf16[16,128,128]{2,1,0:T(8,128)(2,1)}), bf16[16,128,128]{2,1,0:T(8,128)(2,1)}, u32[]{:S(2)}, u32[]{:S(2)}) async-start(bf16[16,128,128]{2,1,0:T(8,128)(2,1)} %copy-done.15), calls=%async_computation.4 | async-start | bytes 1048576 | tf_op jit(solution)/shard_map/back_states/all_to_all | solution.py:175
  373.0 1.2 copy-start.4
  374.2 1.5 copy-start.8
  375.7 1.3 copy-start.12
  377.0 1.2 copy-start.18
  (4 other events, 3.5 us)
Sparse Core Ops, SparseCore 0:
  59.0 11.2 all-gather.8
  72.2 79.0 all-gather.4
  153.4 80.7 all-gather.6
  236.4 75.2 reduce-scatter.2
  314.8 81.1 reduce-scatter.4

commit v2 on v1

--- a/solution.py
+++ b/solution.py
@@ -90,15 +90,17 @@
         state = link[s] * state + x_ref[s].astype(F32)
 
 
-def per_head(kernel, heads, tok, dim, fixed, rows, states, extra_rows, outs, flops):
+def per_head(kernel, heads, tok, dim, fixed, rows, states, extra_rows, outs, flops, first=0):
     smem = pl.BlockSpec(memory_space=pltpu.SMEM)
-    row_spec = pl.BlockSpec((tok, dim), lambda h: (0, h))
-    state_spec = pl.BlockSpec((1, dim, dim), lambda h: (h, 0, 0))
+    row_spec = pl.BlockSpec((tok, dim), lambda h: (0, h + first))
+    state_spec = pl.BlockSpec((1, dim, dim), lambda h: (h + first, 0, 0))
+    row_out = pl.BlockSpec((tok, dim), lambda h: (0, h))
+    state_out = pl.BlockSpec((1, dim, dim), lambda h: (h, 0, 0))
     in_specs = [smem] + [pl.BlockSpec(a.shape, lambda h: (0, 0)) for a in fixed[1:]]
     in_specs += [row_spec] * len(rows) + [state_spec] * len(states) + [row_spec] * len(extra_rows)
     kinds = {
-        "row": (row_spec, jax.ShapeDtypeStruct((tok, heads * dim), BF16)),
-        "state": (state_spec, jax.ShapeDtypeStruct((heads, dim, dim), BF16)),
+        "row": (row_out, jax.ShapeDtypeStruct((tok, heads * dim), BF16)),
+        "state": (state_out, jax.ShapeDtypeStruct((heads, dim, dim), BF16)),
     }
     return pl.pallas_call(
         kernel,
@@ -113,6 +115,19 @@
             transcendentals=heads * tok * tok,
         ),
     )(*fixed, *rows, *states, *extra_rows)
+
+
+def swap(piece, axis, step):
+    count = lax.axis_size(axis)
+    return lax.ppermute(piece, axis, [(i, i ^ step) for i in range(count)])
+
+
+def pick(pieces, index):
+    return lax.dynamic_index_in_dim(jnp.stack(pieces), index, 0, False)
+
+
+def far_first(count):
+    return sorted(range(1, count), key=lambda step: (-bin(step).count("1"), -step))
 
 
 def local(query_rows, key_rows, value_rows, grad_out, out_weight, decay_rates, doc_blocks):
@@ -153,18 +168,29 @@
     one = 2 * tok * dim * dim
     pair = 2 * tok * tok * dim
 
+    groups, plane, halves = (lax.axis_size(name) for name in ("sa", "sb", "head"))
+    here_a, here_b, half = (lax.axis_index(name) for name in ("sa", "sb", "head"))
     with jax.named_scope("grad_columns"):
-        halves = lax.axis_size("head")
         part_rows = tok // halves
-        mine = lax.dynamic_slice_in_dim(grad_out[0], lax.axis_index("head") * part_rows, part_rows)
-        groups = lax.axis_size("sa")
-        width = mine.shape[1] // groups
-        mine = mine.reshape(part_rows, groups, width).transpose(1, 0, 2)
-        mine = lax.all_to_all(mine, "sa", 0, 0, tiled=True)
-        columns = lax.all_gather(mine, "head", axis=0)
-        columns = columns.transpose(1, 0, 2, 3).reshape(groups * tok, width)
+        mine = lax.dynamic_slice_in_dim(grad_out[0], half * part_rows, part_rows)
+        wide = mine.shape[1] // (groups * plane)
+        mine = mine.reshape(part_rows, groups, plane, wide)
+
+        def columns_for(step):
+            rows = lax.dynamic_index_in_dim(mine, here_a ^ step, 1, False)
+            cuts = [lax.dynamic_index_in_dim(rows, here_b ^ d, 1, False) for d in range(plane)]
+            return jnp.concatenate(cuts, axis=1)
+
+        got = {step: swap(columns_for(step), "sa", step) for step in far_first(groups)}
+        got[0] = columns_for(0)
     with jax.named_scope("weight_rows"):
-        weight = lax.all_gather(out_weight, "sb", axis=0, tiled=True)
+        weight = {step: swap(out_weight, "sb", step) for step in far_first(plane)}
+        weight[0] = out_weight
+    with jax.named_scope("grad_columns"):
+        columns = []
+        for step in range(groups):
+            ways = [got[step]] + [swap(got[step], "head", d) for d in range(1, halves)]
+            columns.append(jnp.concatenate([pick(ways, half ^ j) for j in range(halves)], axis=0))
 
     def weights(join, rate):
         return jnp.where(join, jnp.exp(-rate * float(tok)), 0.0)
@@ -189,20 +215,42 @@
             local_state_kernel, heads, tok, dim, fixed[:2], (k, v), (), (), ("state",), one
         )
         state_low = exchanged(local_states, join_fwd, False)
+    cuts = 2 if heads % 2 == 0 else 1
+    share = heads // cuts
     with jax.named_scope("forward"):
-        (normed,) = per_head(
-            forward_kernel, heads, tok, dim, fixed, (q, k, v), (state_low,), (), ("row",),
-            2 * pair + one,
-        )
+        normed = []
+        for c in range(cuts):
+            some = (rates[c * share : (c + 1) * share],) + fixed[1:]
+            normed += per_head(
+                forward_kernel, share, tok, dim, some, (q, k, v), (state_low,), (), ("row",),
+                2 * pair + one, c * share,
+            )
+    with jax.named_scope("normed_group"):
+        group = []
+        for piece in normed:
+            ways = {step: swap(piece, "sa", step) for step in far_first(groups)}
+            group.append(jnp.concatenate([piece] + [ways[d] for d in range(1, groups)], axis=0))
     with jax.named_scope("grad_normed"):
-        partial = jnp.dot(columns, weight, preferred_element_type=F32).astype(BF16)
+        weight = jnp.concatenate([weight[d] for d in range(plane)], axis=0)
+        partial = [
+            jnp.dot(part, weight, preferred_element_type=F32).astype(BF16) for part in columns
+        ]
+        partial = jnp.concatenate([pick(partial, here_a ^ j) for j in range(groups)], axis=0)
         grad_normed = lax.psum_scatter(partial, "sa", scatter_dimension=0, tiled=True)
     with jax.named_scope("grad_weight"):
-        normed_group = lax.all_gather(normed, "sa", axis=0, tiled=True)
-        part = mm(columns, normed_group, 0, 0).astype(BF16)
-        weight_part = lax.psum_scatter(part, "sb", scatter_dimension=0, tiled=True)
+        columns = jnp.concatenate(columns, axis=0)
         norm_factor = (lax.axis_size("dp") * count * tok) ** (-0.5)
-        grad_weight = lax.psum(weight_part, "dp").astype(F32) * norm_factor
+        grad_weight = []
+        for piece in group:
+
+            def term(step):
+                cut = columns[:, step * wide : (step + 1) * wide]
+                return mm(cut, piece, 0, 0).astype(BF16)
+
+            terms = [swap(term(step), "sb", step) for step in far_first(plane)] + [term(0)]
+            total_here = sum(t.astype(F32) for t in terms)
+            grad_weight.append(lax.psum(total_here, "dp") * norm_factor)
+        grad_weight = jnp.concatenate(grad_weight, axis=1)
     with jax.named_scope("back_states"):
         grad_attn, back_local = per_head(
             back_state_kernel, heads, tok, dim, fixed, (q, k, v), (state_low,), (grad_normed,),

time: 410 us -> 396 us (0.966)
  starting transfers between devices: 15.3 us -> 97.6 us
  blocking collectives: 61.7 us -> 0 us
  waiting for transfers between devices: 199 us -> 156 us
  other arithmetic: 9.16 us -> 18.6 us
  local copies, waits for them, and re-layouts: 38 us -> 30.5 us
  matrix products: 22.3 us -> 28.1 us
    ppermute x0 -> x22, waiting for transfers between devices: none -> 108 us  [swap(): return lax.ppermute(piece, axis, [(i, i ^ step) for i in range(count)])]
    all_gather x3 -> x0, waiting for transfers between devices: 90.1 us -> none  [the longest x1 71.8 us: local(): normed_group = lax.all_gather(normed, 'sa', axis=0, tiled=True)]
    ppermute x0 -> x22, starting transfers between devices: none -> 75.8 us  [swap(): return lax.ppermute(piece, axis, [(i, i ^ step) for i in range(count)])]
    reduce_scatter x1, waiting for transfers between devices: 66.1 us -> 0.01 us  [local(): lax.psum_scatter(partial, 'sa', scatter_dimension=0, tiled=True)]
    all_to_all x2 -> x0, blocking collectives: 61.7 us -> none  [the longest x1 43.4 us: local(): mine = lax.all_to_all(mine, 'sa', 0, 0, tiled=True)]
    dot_general x1 -> x8, matrix products: 11.3 us -> 20.8 us  [mm(): lax.dot_general(a, b, (((ca,), (cb,)), ((), ())), preferred_element_type=...]
    all_to_all x1 -> x2, starting transfers between devices: 4.24 us -> 13.5 us  [exchanged(): return lax.all_to_all(done, SEQ, 0, 0, tiled=True).reshape(heads, dim, dim)]
    all_to_all x1 -> x2, waiting for transfers between devices: 13.9 us -> 22.9 us  [exchanged(): return lax.all_to_all(done, SEQ, 0, 0, tiled=True).reshape(heads, dim, dim)]
  transfers between devices with their start and end apart: 8 -> 27, of which waited for: 7 -> 12; matrix products, arithmetic and copies ran while one was open for 9% -> 13% of each run, Pallas kernels for 11% -> 9%
where the time goes in v2:
time: 396 us; the launch traced here: 393 us
  waiting for transfers between devices  156 us (39%)
  starting transfers between devices  97.6 us (25%)
  Pallas kernels  46.1 us (12%)
  local copies, waits for them, and re-layouts  30.5 us (8%)
  matrix products  28.1 us (7%)
  other arithmetic  18.6 us (5%)
  between operations  15.4 us (4%)
    ppermute x22, waiting for transfers between devices, swap(): return lax.ppermute(piece, axis, [(i, i ^ step) for i in range(count)])  108 us
    ppermute x22, starting transfers between devices, swap(): return lax.ppermute(piece, axis, [(i, i ^ step) for i in range(count)])  75.8 us
    pallas_call x5, Pallas kernels, per_head(): pl.pallas_call(kernel, grid=(heads,), in_specs=in_specs, out_specs=[kinds...  42.2 us
    all_to_all x2, waiting for transfers between devices, exchanged(): lax.all_to_all(states.reshape(count, rows, dim), SEQ, 0, 0, tiled=True)  24.9 us
    all_to_all x2, waiting for transfers between devices, exchanged(): return lax.all_to_all(done, SEQ, 0, 0, tiled=True).reshape(heads, dim, dim)  22.9 us
    dot_general x8, matrix products, mm(): lax.dot_general(a, b, (((ca,), (cb,)), ((), ())), preferred_element_type=...  20.8 us
    unnamed x87, local copies, waits for them, and re-layouts  19.1 us
    all_to_all x2, starting transfers between devices, exchanged(): return lax.all_to_all(done, SEQ, 0, 0, tiled=True).reshape(heads, dim, dim)  13.5 us
  transfers between devices with their start and end apart: 27, of which 12 were waited for; matrix products, arithmetic and copies ran while one was open for 13% of the time, Pallas kernels for 9%

profile of v2, /device:TPU:0, one launch (start us, length us, event | category | flops | bytes accessed | tf_op | source)
XLA Modules:
  0.0 392.6 jit_solution(819984853724828799)
XLA Ops:
  30.5 7.8 %collective-permute-done.4 = bf16[128,1536]{1,0:T(8,128)(2,1)S(1)} collective-permute-done((bf16[128,1536]{1,0:T(8,128)(2,1)}, bf16[128,1536]{1,0:T(8,128)(2,1)S(1)}, u32[]{:S(2)}, u32[]{:S(2)}) %collective-permute-start.4) | collective-permute-done | bytes 393248 | tf_op jit(solution)/shard_map/grad_columns/ppermute | solution.py:122
  38.5 16.8 %collective-permute-done.6 = bf16[128,1536]{1,0:T(8,128)(2,1)S(1)} collective-permute-done((bf16[128,1536]{1,0:T(8,128)(2,1)}, bf16[128,1536]{1,0:T(8,128)(2,1)S(1)}, u32[]{:S(2)}, u32[]{:S(2)}) %collective-permute-start.6) | collective-permute-done | bytes 393248 | tf_op jit(solution)/shard_map/grad_columns/ppermute | solution.py:122
  63.9 27.4 %collective-permute-done.3 = bf16[384,2048]{1,0:T(8,128)(2,1)S(1)} collective-permute-done((bf16[384,2048]{1,0:T(8,128)(2,1)S(1)}, bf16[384,2048]{1,0:T(8,128)(2,1)S(1)}, u32[]{:S(2)}, u32[]{:S(2)}) %collective-permute-start.3) | collective-permute-done | bytes 1572896 | tf_op jit(solution)/shard_map/weight_rows/ppermute | solution.py:122
  107.2 6.1 %states.2 = bf16[16,128,128]{2,1,0:T(8,128)(2,1)S(1)} custom-call(f32[16]{0:T(128)S(1)} %copy-done.17, f32[256,4]{1,0:T(8,128)S(1)} %convert_element_type.66.masks, bf16[256,2048]{1,0:T(8,128)(2,1)S(1)} %bitcast.121, bf16[256,2048]{1,0:T(8,128)(2,1)S(1)} %bitcast.126), custom_call_target="tpu_custom_call" | custom-call | flops 134217728 | bytes 3145728 | tf_op jit(solution)/shard_map/states/pallas_call | solution.py:105
  114.1 4.6 %all-to-all-start = ((bf16[16,128,128]{2,1,0:T(8,128)(2,1)}), bf16[16,128,128]{2,1,0:T(8,128)(2,1)}, u32[]{:S(2)}, u32[]{:S(2)}) async-start(bf16[16,128,128]{2,1,0:T(8,128)(2,1)} %copy-done.8), calls=%async_computation | async-start | bytes 1048576 | tf_op jit(solution)/shard_map/states/all_to_all | solution.py:201
  123.0 19.4 %all-to-all-done.x_ref = bf16[16,128,128]{2,1,0:T(8,128)(2,1)} async-done(((bf16[16,128,128]{2,1,0:T(8,128)(2,1)}), bf16[16,128,128]{2,1,0:T(8,128)(2,1)}, u32[]{:S(2)}, u32[]{:S(2)}) %all-to-all-start) | async-done | bytes 524320 | tf_op jit(solution)/shard_map/states/all_to_all | solution.py:201
  144.3 10.0 %all-to-all-start.1 = ((bf16[16,128,128]{2,1,0:T(8,128)(2,1)}), bf16[16,128,128]{2,1,0:T(8,128)(2,1)}, u32[]{:S(2)}, u32[]{:S(2)}) async-start(bf16[16,128,128]{2,1,0:T(8,128)(2,1)} %states.3), calls=%async_computation.1 | async-start | bytes 1048576 | tf_op jit(solution)/shard_map/states/all_to_all | solution.py:211
  155.2 22.9 %all-to-all-done.1.state = bf16[16,128,128]{2,1,0:T(8,128)(2,1)} async-done(((bf16[16,128,128]{2,1,0:T(8,128)(2,1)}), bf16[16,128,128]{2,1,0:T(8,128)(2,1)}, u32[]{:S(2)}, u32[]{:S(2)}) %all-to-all-start.1) | async-done | bytes 524320 | tf_op jit(solution)/shard_map/states/all_to_all | solution.py:211
  178.1 5.6 %forward.3 = bf16[256,1024]{1,0:T(8,128)(2,1)S(1)} custom-call(f32[8]{0:T(128)S(1)} %get-tuple-element.57.rates, f32[256,4]{1,0:T(8,128)S(1)} %convert_element_type.66.masks, f32[256,256]{1,0:T(8,128)S(1)} %fusion.41.allowed, bf16[256,2048]{1,0:T(8,128)(2,1)S(1)} %bitcast.131, bf16[256,2048]{1,0:T(8,128)(2,1)S(1)} %bitcast.122, ...), custom_call_target="tpu_custom_call" | custom-call | flops 335544320 | bytes 2097152 | tf_op jit(solution)/shard_map/forward/pallas_call | solution.py:105
  183.8 3.9 %collective-permute-start.18 = (bf16[256,1024]{1,0:T(8,128)(2,1)S(1)}, bf16[256,1024]{1,0:T(8,128)(2,1)S(1)}, u32[]{:S(2)}, u32[]{:S(2)}) collective-permute-start(bf16[256,1024]{1,0:T(8,128)(2,1)S(1)} %forward.3), channel_id=1, source_target_pairs={{0,24},{8,16},{16,8},{24,0},{1,25},{9,17},{17,9},{25,1},{2,26},{10... | collective-permute-start | bytes 1572872 | tf_op jit(solution)/shard_map/normed_group/ppermute | solution.py:122
  189.4 5.6 %forward.2 = bf16[256,1024]{1,0:T(8,128)(2,1)S(1)} custom-call(f32[8]{0:T(128)S(1)} %get-tuple-element.56.rates, f32[256,4]{1,0:T(8,128)S(1)} %convert_element_type.66.masks, f32[256,256]{1,0:T(8,128)S(1)} %fusion.41.allowed, bf16[256,2048]{1,0:T(8,128)(2,1)S(1)} %bitcast.132, bf16[256,2048]{1,0:T(8,128)(2,1)S(1)} %bitcast.123, ...), custom_call_target="tpu_custom_call" | custom-call | flops 335544320 | bytes 2097152 | tf_op jit(solution)/shard_map/forward/pallas_call | solution.py:105
  195.0 3.5 collective-permute-start.12
  198.5 10.6 %collective-permute-done.18 = bf16[256,1024]{1,0:T(8,128)(2,1)S(1)} collective-permute-done((bf16[256,1024]{1,0:T(8,128)(2,1)S(1)}, bf16[256,1024]{1,0:T(8,128)(2,1)S(1)}, u32[]{:S(2)}, u32[]{:S(2)}) %collective-permute-start.18) | collective-permute-done | bytes 524320 | tf_op jit(solution)/shard_map/normed_group/ppermute | solution.py:122
  209.1 47.7 %collective-permute-start.10 = (bf16[256,1024]{1,0:T(8,128)(2,1)S(1)}, bf16[256,1024]{1,0:T(8,128)(2,1)S(1)}, u32[]{:S(2)}, u32[]{:S(2)}) collective-permute-start(bf16[256,1024]{1,0:T(8,128)(2,1)S(1)} %forward.2), channel_id=1, source_target_pairs={{0,8},{8,0},{16,24},{24,16},{1,9},{9,1},{17,25},{25,17},{2,10},{10... | collective-permute-start | bytes 1572872 | tf_op jit(solution)/shard_map/normed_group/ppermute | solution.py:122
  256.8 10.7 %collective-permute-done.17 = bf16[256,1024]{1,0:T(8,128)(2,1)S(1)} collective-permute-done((bf16[256,1024]{1,0:T(8,128)(2,1)S(1)}, bf16[256,1024]{1,0:T(8,128)(2,1)S(1)}, u32[]{:S(2)}, u32[]{:S(2)}) %collective-permute-start.17) | collective-permute-done | bytes 524320 | tf_op jit(solution)/shard_map/normed_group/ppermute | solution.py:122
  277.1 12.9 %collective-permute-done.11 = bf16[256,1024]{1,0:T(8,128)(2,1)S(1)} collective-permute-done((bf16[256,1024]{1,0:T(8,128)(2,1)S(1)}, bf16[256,1024]{1,0:T(8,128)(2,1)S(1)}, u32[]{:S(2)}, u32[]{:S(2)}) %collective-permute-start.11) | collective-permute-done | bytes 524320 | tf_op jit(solution)/shard_map/normed_group/ppermute | solution.py:122
  294.7 12.9 %back_states.2 = (bf16[256,2048]{1,0:T(8,128)(2,1)S(1)}, bf16[16,128,128]{2,1,0:T(8,128)(2,1)S(1)}) custom-call(f32[16]{0:T(128)S(1)} %copy-done.17, f32[256,4]{1,0:T(8,128)S(1)} %convert_element_type.66.masks, f32[256,256]{1,0:T(8,128)S(1)} %fusion.41.allowed, bf16[256,2048]{1,0:T(8,128)(2,1)S(1)} %bitcast.133, bf16[256,2048]{1,0:T(8,128)(2,1)S(1)} %bitcast.124, ...), custom_call_target="tpu_custom_call" | custom-call | flops 805306368 | bytes 6291456 | tf_op jit(solution)/shard_map/back_states/pallas_call | solution.py:105
  309.4 3.7 all-to-all-start.2
  313.1 3.8 convolution_convert_fusion.10
  325.2 5.5 %all-to-all-done.2.x_ref = bf16[16,128,128]{2,1,0:T(8,128)(2,1)S(1)} async-done(((bf16[16,128,128]{2,1,0:T(8,128)(2,1)}), bf16[16,128,128]{2,1,0:T(8,128)(2,1)S(1)}, u32[]{:S(2)}, u32[]{:S(2)}) %all-to-all-start.2) | async-done | bytes 524320 | tf_op jit(solution)/shard_map/back_states/all_to_all | solution.py:201
  333.4 3.6 all-to-all-start.3
  337.1 3.5 add_multiply_fusion
  340.6 21.2 %collective-permute-done.14 = bf16[384,1024]{1,0:T(8,128)(2,1)} collective-permute-done((bf16[384,1024]{1,0:T(8,128)(2,1)}, bf16[384,1024]{1,0:T(8,128)(2,1)}, u32[]{:S(2)}, u32[]{:S(2)}) %collective-permute-start.14) | collective-permute-done | bytes 786464 | tf_op jit(solution)/shard_map/grad_weight/ppermute | solution.py:122
  373.7 12.0 %grads.1 = (bf16[256,2048]{1,0:T(8,128)(2,1)}, bf16[256,2048]{1,0:T(8,128)(2,1)}, bf16[256,2048]{1,0:T(8,128)(2,1)}) custom-call(f32[16]{0:T(128)S(1)} %copy-done.17, f32[256,4]{1,0:T(8,128)S(1)} %convert_element_type.66.masks, f32[256,256]{1,0:T(8,128)S(1)} %fusion.41.allowed, bf16[256,2048]{1,0:T(8,128)(2,1)S(1)} %bitcast.134, ...), custom_call_target="tpu_custom_call" | custom-call | flops 1744830464 | bytes 7340032 | tf_op jit(solution)/shard_map/grads/pallas_call | solution.py:105
  (196 shorter events, 95.6 us)
Async XLA Ops:
  7.2 286.3 %reduce-scatter.2.cloned.1.call-start = ((), (), s32[]{:S(2)}) async-start(), calls=%async_computation.5 | async-start | bytes 5242880 | tf_op jit(solution)/shard_map/grad_normed/reduce_scatter | solution.py:239
  7.2 53.6 %collective-permute-start.1 = (bf16[384,2048]{1,0:T(8,128)(2,1)}, bf16[384,2048]{1,0:T(8,128)(2,1)}, u32[]{:S(2)}, u32[]{:S(2)}) collective-permute-start(bf16[384,2048]{1,0:T(8,128)(2,1)} %param.11), channel_id=1, source_target_pairs={{0,2},{2,0},{4,6},{6,4},{1,3},{3,1},{5,7},{7,5},{8,10},{10,8},{12,... | collective-permute-start | bytes 4718600 | tf_op jit(solution)/shard_map/weight_rows/ppermute | solution.py:122
  10.2 52.1 %collective-permute-start.2 = (bf16[384,2048]{1,0:T(8,128)(2,1)}, bf16[384,2048]{1,0:T(8,128)(2,1)}, u32[]{:S(2)}, u32[]{:S(2)}) collective-permute-start(bf16[384,2048]{1,0:T(8,128)(2,1)} %param.11), channel_id=1, source_target_pairs={{0,4},{2,6},{4,0},{6,2},{1,5},{3,7},{5,1},{7,3},{8,12},{10,14},{12... | collective-permute-start | bytes 4718600 | tf_op jit(solution)/shard_map/weight_rows/ppermute | solution.py:122
  21.0 17.2 %collective-permute-start.4 = (bf16[128,1536]{1,0:T(8,128)(2,1)}, bf16[128,1536]{1,0:T(8,128)(2,1)S(1)}, u32[]{:S(2)}, u32[]{:S(2)}) collective-permute-start(bf16[128,1536]{1,0:T(8,128)(2,1)} %pad_maximum_fusion.6), channel_id=1, source_target_pairs={{0,8},{8,0},{16,24},{24,16},{1,9},{9,1},{17,25},{25,17},{2,10},{10... | collective-permute-start | bytes 1179656 | tf_op jit(solution)/shard_map/grad_columns/ppermute | solution.py:122
  25.4 30.0 %collective-permute-start.6 = (bf16[128,1536]{1,0:T(8,128)(2,1)}, bf16[128,1536]{1,0:T(8,128)(2,1)S(1)}, u32[]{:S(2)}, u32[]{:S(2)}) collective-permute-start(bf16[128,1536]{1,0:T(8,128)(2,1)} %pad_maximum_fusion.7), channel_id=1, source_target_pairs={{0,16},{8,24},{16,0},{24,8},{1,17},{9,25},{17,1},{25,9},{2,18},{10... | collective-permute-start | bytes 1179656 | tf_op jit(solution)/shard_map/grad_columns/ppermute | solution.py:122
  30.2 26.4 %collective-permute-start.8 = (bf16[128,1536]{1,0:T(8,128)(2,1)S(1)}, bf16[128,1536]{1,0:T(8,128)(2,1)S(1)}, u32[]{:S(2)}, u32[]{:S(2)}) collective-permute-start(bf16[128,1536]{1,0:T(8,128)(2,1)S(1)} %pad_maximum_fusion.8), channel_id=1, source_target_pairs={{0,24},{8,16},{16,8},{24,0},{1,25},{9,17},{17,9},{25,1},{2,26},{10... | collective-permute-start | bytes 1179656 | tf_op jit(solution)/shard_map/grad_columns/ppermute | solution.py:122
  38.2 18.3 %collective-permute-start.5 = (bf16[128,1536]{1,0:T(8,128)(2,1)S(1)}, bf16[128,1536]{1,0:T(8,128)(2,1)S(1)}, u32[]{:S(2)}, u32[]{:S(2)}) collective-permute-start(bf16[128,1536]{1,0:T(8,128)(2,1)S(1)} %collective-permute-done.4), channel_id=1, source_target_pairs={{0,1},{1,0},{2,3},{3,2},{4,5},{5,4},{6,7},{7,6},{8,9},{9,8},{10,11... | collective-permute-start | bytes 1179656 | tf_op jit(solution)/shard_map/grad_columns/ppermute | solution.py:122
  55.3 35.9 %collective-permute-start.3 = (bf16[384,2048]{1,0:T(8,128)(2,1)S(1)}, bf16[384,2048]{1,0:T(8,128)(2,1)S(1)}, u32[]{:S(2)}, u32[]{:S(2)}) collective-permute-start(bf16[384,2048]{1,0:T(8,128)(2,1)S(1)} %copy-done.22), channel_id=1, source_target_pairs={{0,6},{2,4},{4,2},{6,0},{1,7},{3,5},{5,3},{7,1},{8,14},{10,12},{12... | collective-permute-start | bytes 4718600 | tf_op jit(solution)/shard_map/weight_rows/ppermute | solution.py:122
  114.1 28.3 %all-to-all-start = ((bf16[16,128,128]{2,1,0:T(8,128)(2,1)}), bf16[16,128,128]{2,1,0:T(8,128)(2,1)}, u32[]{:S(2)}, u32[]{:S(2)}) async-start(bf16[16,128,128]{2,1,0:T(8,128)(2,1)} %copy-done.8), calls=%async_computation | async-start | bytes 1048576 | tf_op jit(solution)/shard_map/states/all_to_all | solution.py:201
  144.3 33.8 %all-to-all-start.1 = ((bf16[16,128,128]{2,1,0:T(8,128)(2,1)}), bf16[16,128,128]{2,1,0:T(8,128)(2,1)}, u32[]{:S(2)}, u32[]{:S(2)}) async-start(bf16[16,128,128]{2,1,0:T(8,128)(2,1)} %states.3), calls=%async_computation.1 | async-start | bytes 1048576 | tf_op jit(solution)/shard_map/states/all_to_all | solution.py:211
  183.8 25.3 %collective-permute-start.18 = (bf16[256,1024]{1,0:T(8,128)(2,1)S(1)}, bf16[256,1024]{1,0:T(8,128)(2,1)S(1)}, u32[]{:S(2)}, u32[]{:S(2)}) collective-permute-start(bf16[256,1024]{1,0:T(8,128)(2,1)S(1)} %forward.3), channel_id=1, source_target_pairs={{0,24},{8,16},{16,8},{24,0},{1,25},{9,17},{17,9},{25,1},{2,26},{10... | collective-permute-start | bytes 1572872 | tf_op jit(solution)/shard_map/normed_group/ppermute | solution.py:122
  187.7 79.8 %collective-permute-start.17 = (bf16[256,1024]{1,0:T(8,128)(2,1)S(1)}, bf16[256,1024]{1,0:T(8,128)(2,1)S(1)}, u32[]{:S(2)}, u32[]{:S(2)}) collective-permute-start(bf16[256,1024]{1,0:T(8,128)(2,1)S(1)} %forward.3), channel_id=1, source_target_pairs={{0,16},{8,24},{16,0},{24,8},{1,17},{9,25},{17,1},{25,9},{2,18},{10... | collective-permute-start | bytes 1572872 | tf_op jit(solution)/shard_map/normed_group/ppermute | solution.py:122
  188.7 78.9 %collective-permute-start.16 = (bf16[256,1024]{1,0:T(8,128)(2,1)S(1)}, bf16[256,1024]{1,0:T(8,128)(2,1)S(1)}, u32[]{:S(2)}, u32[]{:S(2)}) collective-permute-start(bf16[256,1024]{1,0:T(8,128)(2,1)S(1)} %forward.3), channel_id=1, source_target_pairs={{0,8},{8,0},{16,24},{24,16},{1,9},{9,1},{17,25},{25,17},{2,10},{10... | collective-permute-start | bytes 1572872 | tf_op jit(solution)/shard_map/normed_group/ppermute | solution.py:122
  195.0 82.0 %collective-permute-start.12 = (bf16[256,1024]{1,0:T(8,128)(2,1)S(1)}, bf16[256,1024]{1,0:T(8,128)(2,1)S(1)}, u32[]{:S(2)}, u32[]{:S(2)}) collective-permute-start(bf16[256,1024]{1,0:T(8,128)(2,1)S(1)} %forward.2), channel_id=1, source_target_pairs={{0,24},{8,16},{16,8},{24,0},{1,25},{9,17},{17,9},{25,1},{2,26},{10... | collective-permute-start | bytes 1572872 | tf_op jit(solution)/shard_map/normed_group/ppermute | solution.py:122
  198.4 91.5 %collective-permute-start.11 = (bf16[256,1024]{1,0:T(8,128)(2,1)S(1)}, bf16[256,1024]{1,0:T(8,128)(2,1)S(1)}, u32[]{:S(2)}, u32[]{:S(2)}) collective-permute-start(bf16[256,1024]{1,0:T(8,128)(2,1)S(1)} %forward.2), channel_id=1, source_target_pairs={{0,16},{8,24},{16,0},{24,8},{1,17},{9,25},{17,1},{25,9},{2,18},{10... | collective-permute-start | bytes 1572872 | tf_op jit(solution)/shard_map/normed_group/ppermute | solution.py:122
  209.1 80.9 %collective-permute-start.10 = (bf16[256,1024]{1,0:T(8,128)(2,1)S(1)}, bf16[256,1024]{1,0:T(8,128)(2,1)S(1)}, u32[]{:S(2)}, u32[]{:S(2)}) collective-permute-start(bf16[256,1024]{1,0:T(8,128)(2,1)S(1)} %forward.2), channel_id=1, source_target_pairs={{0,8},{8,0},{16,24},{24,16},{1,9},{9,1},{17,25},{25,17},{2,10},{10... | collective-permute-start | bytes 1572872 | tf_op jit(solution)/shard_map/normed_group/ppermute | solution.py:122
  269.4 52.4 %collective-permute-start.21 = (bf16[384,1024]{1,0:T(8,128)(2,1)}, bf16[384,1024]{1,0:T(8,128)(2,1)}, u32[]{:S(2)}, u32[]{:S(2)}) collective-permute-start(bf16[384,1024]{1,0:T(8,128)(2,1)} %convolution_convert_fusion.5), channel_id=1, source_target_pairs={{0,2},{2,0},{4,6},{6,4},{1,3},{3,1},{5,7},{7,5},{8,10},{10,8},{12,... | collective-permute-start | bytes 2359304 | tf_op jit(solution)/shard_map/grad_weight/ppermute | solution.py:122
  273.0 64.0 %collective-permute-start.20 = (bf16[384,1024]{1,0:T(8,128)(2,1)}, bf16[384,1024]{1,0:T(8,128)(2,1)}, u32[]{:S(2)}, u32[]{:S(2)}) collective-permute-start(bf16[384,1024]{1,0:T(8,128)(2,1)} %convolution_convert_fusion.6), channel_id=1, source_target_pairs={{0,4},{2,6},{4,0},{6,2},{1,5},{3,7},{5,1},{7,3},{8,12},{10,14},{12... | collective-permute-start | bytes 2359304 | tf_op jit(solution)/shard_map/grad_weight/ppermute | solution.py:122
  277.0 60.0 %collective-permute-start.19 = (bf16[384,1024]{1,0:T(8,128)(2,1)}, bf16[384,1024]{1,0:T(8,128)(2,1)}, u32[]{:S(2)}, u32[]{:S(2)}) collective-permute-start(bf16[384,1024]{1,0:T(8,128)(2,1)} %convolution_convert_fusion.7), channel_id=1, source_target_pairs={{0,6},{2,4},{4,2},{6,0},{1,7},{3,5},{5,3},{7,1},{8,14},{10,12},{12... | collective-permute-start | bytes 2359304 | tf_op jit(solution)/shard_map/grad_weight/ppermute | solution.py:122
  291.8 48.7 %collective-permute-start.15 = (bf16[384,1024]{1,0:T(8,128)(2,1)}, bf16[384,1024]{1,0:T(8,128)(2,1)}, u32[]{:S(2)}, u32[]{:S(2)}) collective-permute-start(bf16[384,1024]{1,0:T(8,128)(2,1)} %convolution_convert_fusion.9), channel_id=1, source_target_pairs={{0,2},{2,0},{4,6},{6,4},{1,3},{3,1},{5,7},{7,5},{8,10},{10,8},{12,... | collective-permute-start | bytes 2359304 | tf_op jit(solution)/shard_map/grad_weight/ppermute | solution.py:122
  309.4 21.3 %all-to-all-start.2 = ((bf16[16,128,128]{2,1,0:T(8,128)(2,1)}), bf16[16,128,128]{2,1,0:T(8,128)(2,1)S(1)}, u32[]{:S(2)}, u32[]{:S(2)}) async-start(bf16[16,128,128]{2,1,0:T(8,128)(2,1)} %copy-done.16), calls=%async_computation.3 | async-start | bytes 1048576 | tf_op jit(solution)/shard_map/back_states/all_to_all | solution.py:201
  316.9 44.9 %collective-permute-start.14 = (bf16[384,1024]{1,0:T(8,128)(2,1)}, bf16[384,1024]{1,0:T(8,128)(2,1)}, u32[]{:S(2)}, u32[]{:S(2)}) collective-permute-start(bf16[384,1024]{1,0:T(8,128)(2,1)} %convolution_convert_fusion.10), channel_id=1, source_target_pairs={{0,4},{2,6},{4,0},{6,2},{1,5},{3,7},{5,1},{7,3},{8,12},{10,14},{12... | collective-permute-start | bytes 2359304 | tf_op jit(solution)/shard_map/grad_weight/ppermute | solution.py:122
  321.9 39.9 %collective-permute-start.13 = (bf16[384,1024]{1,0:T(8,128)(2,1)}, bf16[384,1024]{1,0:T(8,128)(2,1)}, u32[]{:S(2)}, u32[]{:S(2)}) collective-permute-start(bf16[384,1024]{1,0:T(8,128)(2,1)} %convolution_convert_fusion.11), channel_id=1, source_target_pairs={{0,6},{2,4},{4,2},{6,0},{1,7},{3,5},{5,3},{7,1},{8,14},{10,12},{12... | collective-permute-start | bytes 2359304 | tf_op jit(solution)/shard_map/grad_weight/ppermute | solution.py:122
  333.4 33.4 %all-to-all-start.3 = ((bf16[16,128,128]{2,1,0:T(8,128)(2,1)}), bf16[16,128,128]{2,1,0:T(8,128)(2,1)S(1)}, u32[]{:S(2)}, u32[]{:S(2)}) async-start(bf16[16,128,128]{2,1,0:T(8,128)(2,1)} %back_states.3), calls=%async_computation.4 | async-start | bytes 1048576 | tf_op jit(solution)/shard_map/back_states/all_to_all | solution.py:211
  (42 other events, 681.4 us)
Sparse Core Ops, SparseCore 0:
  102.3 105.3 reduce-scatter.1

commit v3 on v2

--- a/solution.py
+++ b/solution.py
@@ -170,36 +170,17 @@
 
     groups, plane, halves = (lax.axis_size(name) for name in ("sa", "sb", "head"))
     here_a, here_b, half = (lax.axis_index(name) for name in ("sa", "sb", "head"))
-    with jax.named_scope("grad_columns"):
-        part_rows = tok // halves
-        mine = lax.dynamic_slice_in_dim(grad_out[0], half * part_rows, part_rows)
-        wide = mine.shape[1] // (groups * plane)
-        mine = mine.reshape(part_rows, groups, plane, wide)
-
-        def columns_for(step):
-            rows = lax.dynamic_index_in_dim(mine, here_a ^ step, 1, False)
-            cuts = [lax.dynamic_index_in_dim(rows, here_b ^ d, 1, False) for d in range(plane)]
-            return jnp.concatenate(cuts, axis=1)
-
-        got = {step: swap(columns_for(step), "sa", step) for step in far_first(groups)}
-        got[0] = columns_for(0)
-    with jax.named_scope("weight_rows"):
-        weight = {step: swap(out_weight, "sb", step) for step in far_first(plane)}
-        weight[0] = out_weight
-    with jax.named_scope("grad_columns"):
-        columns = []
-        for step in range(groups):
-            ways = [got[step]] + [swap(got[step], "head", d) for d in range(1, halves)]
-            columns.append(jnp.concatenate([pick(ways, half ^ j) for j in range(halves)], axis=0))
-
     def weights(join, rate):
         return jnp.where(join, jnp.exp(-rate * float(tok)), 0.0)
 
-    def exchanged(states, join, backward):
+    def send_parts(states):
         rows = heads * dim // count
         assert dim % rows == 0
-        parts = lax.all_to_all(states.reshape(count, rows, dim), SEQ, 0, 0, tiled=True)
-        done = pl.pallas_call(
+        return lax.all_to_all(states.reshape(count, rows, dim), SEQ, 0, 0, tiled=True)
+
+    def scan_parts(parts, join, backward):
+        rows = parts.shape[1]
+        return pl.pallas_call(
             functools.partial(scan_kernel, backward),
             in_specs=[
                 pl.BlockSpec(memory_space=pltpu.SMEM),
@@ -208,13 +189,41 @@
             out_specs=pl.BlockSpec(memory_space=pltpu.VMEM),
             out_shape=jax.ShapeDtypeStruct(parts.shape, BF16),
         )(weights(join, rates[span * rows // dim]), parts)
-        return lax.all_to_all(done, SEQ, 0, 0, tiled=True).reshape(heads, dim, dim)
-
+
+    def send_back(scanned):
+        return lax.all_to_all(scanned, SEQ, 0, 0, tiled=True).reshape(heads, dim, dim)
+
+    with jax.named_scope("weight_rows"):
+        weight = {step: swap(out_weight, "sb", step) for step in far_first(plane)}
+        weight[0] = out_weight
     with jax.named_scope("states"):
         (local_states,) = per_head(
             local_state_kernel, heads, tok, dim, fixed[:2], (k, v), (), (), ("state",), one
         )
-        state_low = exchanged(local_states, join_fwd, False)
+    with jax.named_scope("grad_columns"):
+        part_rows = tok // halves
+        grads_in, _ = lax.optimization_barrier((grad_out[0], local_states))
+        mine = lax.dynamic_slice_in_dim(grads_in, half * part_rows, part_rows)
+        wide = mine.shape[1] // (groups * plane)
+        mine = mine.reshape(part_rows, groups, plane, wide)
+
+        def columns_for(step):
+            rows = lax.dynamic_index_in_dim(mine, here_a ^ step, 1, False)
+            cuts = [lax.dynamic_index_in_dim(rows, here_b ^ d, 1, False) for d in range(plane)]
+            return jnp.concatenate(cuts, axis=1)
+
+        got = {step: swap(columns_for(step), "sa", step) for step in far_first(groups)}
+        got[0] = columns_for(0)
+    with jax.named_scope("states"):
+        scanned = scan_parts(send_parts(local_states), join_fwd, False)
+        _, got = lax.optimization_barrier((scanned, got))
+        state_low = send_back(scanned)
+    with jax.named_scope("grad_columns"):
+        columns = []
+        for step in range(groups):
+            ways = [got[step]] + [swap(got[step], "head", d) for d in range(1, halves)]
+            columns.append(jnp.concatenate([pick(ways, half ^ j) for j in range(halves)], axis=0))
+
     cuts = 2 if heads % 2 == 0 else 1
     share = heads // cuts
     with jax.named_scope("forward"):
@@ -231,6 +240,7 @@
             ways = {step: swap(piece, "sa", step) for step in far_first(groups)}
             group.append(jnp.concatenate([piece] + [ways[d] for d in range(1, groups)], axis=0))
     with jax.named_scope("grad_normed"):
+        columns, weight, _ = lax.optimization_barrier((columns, weight, normed))
         weight = jnp.concatenate([weight[d] for d in range(plane)], axis=0)
         partial = [
             jnp.dot(part, weight, preferred_element_type=F32).astype(BF16) for part in columns
@@ -256,7 +266,7 @@
             back_state_kernel, heads, tok, dim, fixed, (q, k, v), (state_low,), (grad_normed,),
             ("row", "state"), 2 * pair + 2 * one,
         )
-        back_low = exchanged(back_local, join_rev, True)
+        back_low = send_back(scan_parts(send_parts(back_local), join_rev, True))
     with jax.named_scope("grads"):
         grads = per_head(
             grads_kernel, heads, tok, dim, fixed, (q, k, v), (state_low, back_low), (grad_attn,),

time: 396 us -> 391 us (0.987)
  starting transfers between devices: 97.6 us -> 89.6 us
    all_to_all x4, waiting for transfers between devices: 47.8 us -> 13.2 us  [the longest x2 9.4 us: send_back(): lax.all_to_all(scanned, SEQ, 0, 0, tiled=True).reshape(heads, dim, dim)]
    ppermute x22, waiting for transfers between devices: 108 us -> 143 us  [swap(): return lax.ppermute(piece, axis, [(i, i ^ step) for i in range(count)])]
    ppermute x22, starting transfers between devices: 75.8 us -> 64 us  [swap(): return lax.ppermute(piece, axis, [(i, i ^ step) for i in range(count)])]
    concatenate x3 -> x4, other arithmetic: 4.28 us -> 0.14 us  [columns_for(): return jnp.concatenate(cuts, axis=1)]
    unnamed x87 -> x92, local copies, waits for them, and re-layouts: 19.1 us -> 19.4 us
  transfers between devices with their start and end apart: 27 -> 27, of which waited for: 12 -> 9; matrix products, arithmetic and copies ran while one was open for 13% -> 13% of each run, Pallas kernels for 9% -> 10%
where the time goes in v3:
time: 391 us; the launch traced here: 387 us
  waiting for transfers between devices  156 us (40%)
  starting transfers between devices  89.6 us (23%)
  Pallas kernels  49 us (13%)
  local copies, waits for them, and re-layouts  29.8 us (8%)
  matrix products  28.2 us (7%)
  other arithmetic  18.4 us (5%)
  between operations  15.6 us (4%)
    ppermute x22, waiting for transfers between devices, swap(): return lax.ppermute(piece, axis, [(i, i ^ step) for i in range(count)])  143 us
    ppermute x22, starting transfers between devices, swap(): return lax.ppermute(piece, axis, [(i, i ^ step) for i in range(count)])  64 us
    pallas_call x5, Pallas kernels, per_head(): pl.pallas_call(kernel, grid=(heads,), in_specs=in_specs, out_specs=[kinds...  45.1 us
    dot_general x8, matrix products, mm(): lax.dot_general(a, b, (((ca,), (cb,)), ((), ())), preferred_element_type=...  21 us
    unnamed x92, local copies, waits for them, and re-layouts  19.4 us
    all_to_all x2, starting transfers between devices, send_back(): lax.all_to_all(scanned, SEQ, 0, 0, tiled=True).reshape(heads, dim, dim)  16.3 us
    all_to_all x2, waiting for transfers between devices, send_back(): lax.all_to_all(scanned, SEQ, 0, 0, tiled=True).reshape(heads, dim, dim)  9.4 us
    all_to_all x2, starting transfers between devices, send_parts(): lax.all_to_all(states.reshape(count, rows, dim), SEQ, 0, 0, tiled=True)  9.27 us
  transfers between devices with their start and end apart: 27, of which 9 were waited for; matrix products, arithmetic and copies ran while one was open for 13% of the time, Pallas kernels for 10%

profile of v3, /device:TPU:0, one launch (start us, length us, event | category | flops | bytes accessed | tf_op | source)
XLA Modules:
  0.0 386.6 jit_solution(12100977938574505282)
XLA Ops:
  7.2 3.0 collective-permute-start.7
  20.6 8.5 %states.2 = bf16[16,128,128]{2,1,0:T(8,128)(2,1)} custom-call(f32[16]{0:T(128)S(1)} %copy-done.13, f32[256,4]{1,0:T(8,128)S(1)} %convert_element_type.66.masks, bf16[256,2048]{1,0:T(8,128)(2,1)S(1)} %bitcast.117, bf16[256,2048]{1,0:T(8,128)(2,1)S(1)} %bitcast.122), custom_call_target="tpu_custom_call" | custom-call | flops 134217728 | bytes 3145728 | tf_op jit(solution)/shard_map/states/pallas_call | solution.py:105
  29.1 5.0 %all-to-all-start = ((bf16[16,128,128]{2,1,0:T(8,128)(2,1)}), bf16[16,128,128]{2,1,0:T(8,128)(2,1)}, u32[]{:S(2)}, u32[]{:S(2)}) async-start(bf16[16,128,128]{2,1,0:T(8,128)(2,1)} %states.2), calls=%async_computation | async-start | bytes 1048576 | tf_op jit(solution)/shard_map/states/all_to_all | solution.py:179
  34.2 3.2 copy.37
  48.8 3.1 all-to-all-done.x_ref
  53.9 5.4 %collective-permute-done = bf16[128,1536]{1,0:T(8,128)(2,1)S(1)} collective-permute-done((bf16[128,1536]{1,0:T(8,128)(2,1)S(1)}, bf16[128,1536]{1,0:T(8,128)(2,1)S(1)}, u32[]{:S(2)}, u32[]{:S(2)}) %collective-permute-start) | collective-permute-done | bytes 393248 | tf_op jit(solution)/shard_map/grad_columns/ppermute | solution.py:122
  61.7 12.6 %collective-permute-done.1 = bf16[128,1536]{1,0:T(8,128)(2,1)S(1)} collective-permute-done((bf16[128,1536]{1,0:T(8,128)(2,1)S(1)}, bf16[128,1536]{1,0:T(8,128)(2,1)S(1)}, u32[]{:S(2)}, u32[]{:S(2)}) %collective-permute-start.1) | collective-permute-done | bytes 393248 | tf_op jit(solution)/shard_map/grad_columns/ppermute | solution.py:122
  74.4 11.3 %all-to-all-start.1 = ((bf16[16,128,128]{2,1,0:T(8,128)(2,1)}), bf16[16,128,128]{2,1,0:T(8,128)(2,1)}, u32[]{:S(2)}, u32[]{:S(2)}) async-start(bf16[16,128,128]{2,1,0:T(8,128)(2,1)} %states.3), calls=%async_computation.1 | async-start | bytes 1048576 | tf_op jit(solution)/shard_map/states/all_to_all | solution.py:194
  93.6 9.4 %all-to-all-done.1.state = bf16[16,128,128]{2,1,0:T(8,128)(2,1)} async-done(((bf16[16,128,128]{2,1,0:T(8,128)(2,1)}), bf16[16,128,128]{2,1,0:T(8,128)(2,1)}, u32[]{:S(2)}, u32[]{:S(2)}) %all-to-all-start.1) | async-done | bytes 524320 | tf_op jit(solution)/shard_map/states/all_to_all | solution.py:194
  103.1 5.8 %forward.2 = bf16[256,1024]{1,0:T(8,128)(2,1)S(1)} custom-call(f32[8]{0:T(128)S(1)} %get-tuple-element.73.rates, f32[256,4]{1,0:T(8,128)S(1)} %convert_element_type.66.masks, f32[256,256]{1,0:T(8,128)S(1)} %fusion.29.allowed, bf16[256,2048]{1,0:T(8,128)(2,1)S(1)} %bitcast.127, bf16[256,2048]{1,0:T(8,128)(2,1)S(1)} %bitcast.118, ...), custom_call_target="tpu_custom_call" | custom-call | flops 335544320 | bytes 2097152 | tf_op jit(solution)/shard_map/forward/pallas_call | solution.py:105
  109.6 5.6 %forward.3 = bf16[256,1024]{1,0:T(8,128)(2,1)S(1)} custom-call(f32[8]{0:T(128)S(1)} %get-tuple-element.72.rates, f32[256,4]{1,0:T(8,128)S(1)} %convert_element_type.66.masks, f32[256,256]{1,0:T(8,128)S(1)} %fusion.29.allowed, bf16[256,2048]{1,0:T(8,128)(2,1)S(1)} %bitcast.128, bf16[256,2048]{1,0:T(8,128)(2,1)S(1)} %bitcast.119, ...), custom_call_target="tpu_custom_call" | custom-call | flops 335544320 | bytes 2097152 | tf_op jit(solution)/shard_map/forward/pallas_call | solution.py:105
  141.7 16.8 %collective-permute-done.18 = bf16[256,1024]{1,0:T(8,128)(2,1)S(1)} collective-permute-done((bf16[256,1024]{1,0:T(8,128)(2,1)}, bf16[256,1024]{1,0:T(8,128)(2,1)S(1)}, u32[]{:S(2)}, u32[]{:S(2)}) %collective-permute-start.18) | collective-permute-done | bytes 524320 | tf_op jit(solution)/shard_map/normed_group/ppermute | solution.py:122
  158.5 38.0 %collective-permute-start.10 = (bf16[256,1024]{1,0:T(8,128)(2,1)S(1)}, bf16[256,1024]{1,0:T(8,128)(2,1)S(1)}, u32[]{:S(2)}, u32[]{:S(2)}) collective-permute-start(bf16[256,1024]{1,0:T(8,128)(2,1)S(1)} %copy-done.7), channel_id=1, source_target_pairs={{0,8},{8,0},{16,24},{24,16},{1,9},{9,1},{17,25},{25,17},{2,10},{10... | collective-permute-start | bytes 1572872 | tf_op jit(solution)/shard_map/normed_group/ppermute | solution.py:122
  196.5 57.1 %collective-permute-done.17 = bf16[256,1024]{1,0:T(8,128)(2,1)S(1)} collective-permute-done((bf16[256,1024]{1,0:T(8,128)(2,1)}, bf16[256,1024]{1,0:T(8,128)(2,1)S(1)}, u32[]{:S(2)}, u32[]{:S(2)}) %collective-permute-start.17) | collective-permute-done | bytes 524320 | tf_op jit(solution)/shard_map/normed_group/ppermute | solution.py:122
  262.7 28.5 %collective-permute-done.11 = bf16[256,1024]{1,0:T(8,128)(2,1)S(1)} collective-permute-done((bf16[256,1024]{1,0:T(8,128)(2,1)}, bf16[256,1024]{1,0:T(8,128)(2,1)S(1)}, u32[]{:S(2)}, u32[]{:S(2)}) %collective-permute-start.11) | collective-permute-done | bytes 524320 | tf_op jit(solution)/shard_map/normed_group/ppermute | solution.py:122
  295.3 12.9 %back_states.2 = (bf16[256,2048]{1,0:T(8,128)(2,1)S(1)}, bf16[16,128,128]{2,1,0:T(8,128)(2,1)S(1)}) custom-call(f32[16]{0:T(128)S(1)} %copy-done.14, f32[256,4]{1,0:T(8,128)S(1)} %convert_element_type.66.masks, f32[256,256]{1,0:T(8,128)S(1)} %fusion.29.allowed, bf16[256,2048]{1,0:T(8,128)(2,1)S(1)} %bitcast.129, bf16[256,2048]{1,0:T(8,128)(2,1)S(1)} %bitcast.120, ...), custom_call_target="tpu_custom_call" | custom-call | flops 805306368 | bytes 6291456 | tf_op jit(solution)/shard_map/back_states/pallas_call | solution.py:105
  310.0 4.2 %all-to-all-start.2 = ((bf16[16,128,128]{2,1,0:T(8,128)(2,1)}), bf16[16,128,128]{2,1,0:T(8,128)(2,1)}, u32[]{:S(2)}, u32[]{:S(2)}) async-start(bf16[16,128,128]{2,1,0:T(8,128)(2,1)} %copy-done.12), calls=%async_computation.3 | async-start | bytes 1048576 | tf_op jit(solution)/shard_map/back_states/all_to_all | solution.py:179
  314.2 3.8 convolution_convert_fusion.10
  319.8 3.0 convolution_convert_fusion.11
  330.0 5.0 %all-to-all-start.3 = ((bf16[16,128,128]{2,1,0:T(8,128)(2,1)}), bf16[16,128,128]{2,1,0:T(8,128)(2,1)}, u32[]{:S(2)}, u32[]{:S(2)}) async-start(bf16[16,128,128]{2,1,0:T(8,128)(2,1)} %back_states.3), calls=%async_computation.4 | async-start | bytes 1048576 | tf_op jit(solution)/shard_map/back_states/all_to_all | solution.py:194
  335.1 3.7 add_multiply_fusion
  338.8 22.4 %collective-permute-done.14 = bf16[384,1024]{1,0:T(8,128)(2,1)} collective-permute-done((bf16[384,1024]{1,0:T(8,128)(2,1)}, bf16[384,1024]{1,0:T(8,128)(2,1)}, u32[]{:S(2)}, u32[]{:S(2)}) %collective-permute-start.14) | collective-permute-done | bytes 786464 | tf_op jit(solution)/shard_map/grad_weight/ppermute | solution.py:122
  361.2 3.0 add_multiply_fusion.1
  367.4 12.3 %grads.1 = (bf16[256,2048]{1,0:T(8,128)(2,1)}, bf16[256,2048]{1,0:T(8,128)(2,1)}, bf16[256,2048]{1,0:T(8,128)(2,1)}) custom-call(f32[16]{0:T(128)S(1)} %copy-done.14, f32[256,4]{1,0:T(8,128)S(1)} %convert_element_type.66.masks, f32[256,256]{1,0:T(8,128)S(1)} %fusion.29.allowed, bf16[256,2048]{1,0:T(8,128)(2,1)S(1)} %bitcast.130, ...), custom_call_target="tpu_custom_call" | custom-call | flops 1744830464 | bytes 7340032 | tf_op jit(solution)/shard_map/grads/pallas_call | solution.py:105
  (202 shorter events, 87.4 us)
Async XLA Ops:
  7.2 108.1 %collective-permute-start.7 = (bf16[384,2048]{1,0:T(8,128)(2,1)}, bf16[384,2048]{1,0:T(8,128)(2,1)}, u32[]{:S(2)}, u32[]{:S(2)}) collective-permute-start(bf16[384,2048]{1,0:T(8,128)(2,1)} %param.11), channel_id=1, source_target_pairs={{0,2},{2,0},{4,6},{6,4},{1,3},{3,1},{5,7},{7,5},{8,10},{10,8},{12,... | collective-permute-start | bytes 4718600 | tf_op jit(solution)/shard_map/weight_rows/ppermute | solution.py:122
  10.2 105.1 %collective-permute-start.8 = (bf16[384,2048]{1,0:T(8,128)(2,1)}, bf16[384,2048]{1,0:T(8,128)(2,1)}, u32[]{:S(2)}, u32[]{:S(2)}) collective-permute-start(bf16[384,2048]{1,0:T(8,128)(2,1)} %param.11), channel_id=1, source_target_pairs={{0,4},{2,6},{4,0},{6,2},{1,5},{3,7},{5,1},{7,3},{8,12},{10,14},{12... | collective-permute-start | bytes 4718600 | tf_op jit(solution)/shard_map/weight_rows/ppermute | solution.py:122
  29.1 22.9 %all-to-all-start = ((bf16[16,128,128]{2,1,0:T(8,128)(2,1)}), bf16[16,128,128]{2,1,0:T(8,128)(2,1)}, u32[]{:S(2)}, u32[]{:S(2)}) async-start(bf16[16,128,128]{2,1,0:T(8,128)(2,1)} %states.2), calls=%async_computation | async-start | bytes 1048576 | tf_op jit(solution)/shard_map/states/all_to_all | solution.py:179
  38.3 21.0 %collective-permute-start = (bf16[128,1536]{1,0:T(8,128)(2,1)S(1)}, bf16[128,1536]{1,0:T(8,128)(2,1)S(1)}, u32[]{:S(2)}, u32[]{:S(2)}) collective-permute-start(bf16[128,1536]{1,0:T(8,128)(2,1)S(1)} %pad_maximum_fusion.10), channel_id=1, source_target_pairs={{0,8},{8,0},{16,24},{24,16},{1,9},{9,1},{17,25},{25,17},{2,10},{10... | collective-permute-start | bytes 1179656 | tf_op jit(solution)/shard_map/grad_columns/ppermute | solution.py:122
  40.7 33.5 %collective-permute-start.1 = (bf16[128,1536]{1,0:T(8,128)(2,1)S(1)}, bf16[128,1536]{1,0:T(8,128)(2,1)S(1)}, u32[]{:S(2)}, u32[]{:S(2)}) collective-permute-start(bf16[128,1536]{1,0:T(8,128)(2,1)S(1)} %pad_maximum_fusion.11), channel_id=1, source_target_pairs={{0,16},{8,24},{16,0},{24,8},{1,17},{9,25},{17,1},{25,9},{2,18},{10... | collective-permute-start | bytes 1179656 | tf_op jit(solution)/shard_map/grad_columns/ppermute | solution.py:122
  43.7 30.5 %collective-permute-start.2 = (bf16[128,1536]{1,0:T(8,128)(2,1)S(1)}, bf16[128,1536]{1,0:T(8,128)(2,1)}, u32[]{:S(2)}, u32[]{:S(2)}) collective-permute-start(bf16[128,1536]{1,0:T(8,128)(2,1)S(1)} %pad_maximum_fusion.12), channel_id=1, source_target_pairs={{0,24},{8,16},{16,8},{24,0},{1,25},{9,17},{17,9},{25,1},{2,26},{10... | collective-permute-start | bytes 1179656 | tf_op jit(solution)/shard_map/grad_columns/ppermute | solution.py:122
  59.3 56.0 %collective-permute-start.9 = (bf16[384,2048]{1,0:T(8,128)(2,1)}, bf16[384,2048]{1,0:T(8,128)(2,1)}, u32[]{:S(2)}, u32[]{:S(2)}) collective-permute-start(bf16[384,2048]{1,0:T(8,128)(2,1)} %param.11), channel_id=1, source_target_pairs={{0,6},{2,4},{4,2},{6,0},{1,7},{3,5},{5,3},{7,1},{8,14},{10,12},{12... | collective-permute-start | bytes 4718600 | tf_op jit(solution)/shard_map/weight_rows/ppermute | solution.py:122
  74.3 11.8 %collective-permute-start.3 = (bf16[128,1536]{1,0:T(8,128)(2,1)S(1)}, bf16[128,1536]{1,0:T(8,128)(2,1)S(1)}, u32[]{:S(2)}, u32[]{:S(2)}) collective-permute-start(bf16[128,1536]{1,0:T(8,128)(2,1)S(1)} %pad_maximum_fusion.9), channel_id=1, source_target_pairs={{0,1},{1,0},{2,3},{3,2},{4,5},{5,4},{6,7},{7,6},{8,9},{9,8},{10,11... | collective-permute-start | bytes 1179656 | tf_op jit(solution)/shard_map/grad_columns/ppermute | solution.py:122
  74.4 28.6 %all-to-all-start.1 = ((bf16[16,128,128]{2,1,0:T(8,128)(2,1)}), bf16[16,128,128]{2,1,0:T(8,128)(2,1)}, u32[]{:S(2)}, u32[]{:S(2)}) async-start(bf16[16,128,128]{2,1,0:T(8,128)(2,1)} %states.3), calls=%async_computation.1 | async-start | bytes 1048576 | tf_op jit(solution)/shard_map/states/all_to_all | solution.py:194
  85.7 208.4 %reduce-scatter.2.cloned.1.call-start = ((), (), s32[]{:S(2)}) async-start(), calls=%async_computation.5 | async-start | bytes 5242880 | tf_op jit(solution)/shard_map/grad_normed/reduce_scatter | solution.py:249
  133.1 25.4 %collective-permute-start.18 = (bf16[256,1024]{1,0:T(8,128)(2,1)}, bf16[256,1024]{1,0:T(8,128)(2,1)S(1)}, u32[]{:S(2)}, u32[]{:S(2)}) collective-permute-start(bf16[256,1024]{1,0:T(8,128)(2,1)} %copy-done.10), channel_id=1, source_target_pairs={{0,24},{8,16},{16,8},{24,0},{1,25},{9,17},{17,9},{25,1},{2,26},{10... | collective-permute-start | bytes 1572872 | tf_op jit(solution)/shard_map/normed_group/ppermute | solution.py:122
  134.7 118.8 %collective-permute-start.17 = (bf16[256,1024]{1,0:T(8,128)(2,1)}, bf16[256,1024]{1,0:T(8,128)(2,1)S(1)}, u32[]{:S(2)}, u32[]{:S(2)}) collective-permute-start(bf16[256,1024]{1,0:T(8,128)(2,1)} %copy-done.10), channel_id=1, source_target_pairs={{0,16},{8,24},{16,0},{24,8},{1,17},{9,25},{17,1},{25,9},{2,18},{10... | collective-permute-start | bytes 1572872 | tf_op jit(solution)/shard_map/normed_group/ppermute | solution.py:122
  134.7 118.8 %collective-permute-start.16 = (bf16[256,1024]{1,0:T(8,128)(2,1)}, bf16[256,1024]{1,0:T(8,128)(2,1)S(1)}, u32[]{:S(2)}, u32[]{:S(2)}) collective-permute-start(bf16[256,1024]{1,0:T(8,128)(2,1)} %copy-done.10), channel_id=1, source_target_pairs={{0,8},{8,0},{16,24},{24,16},{1,9},{9,1},{17,25},{25,17},{2,10},{10... | collective-permute-start | bytes 1572872 | tf_op jit(solution)/shard_map/normed_group/ppermute | solution.py:122
  137.5 124.3 %collective-permute-start.12 = (bf16[256,1024]{1,0:T(8,128)(2,1)}, bf16[256,1024]{1,0:T(8,128)(2,1)S(1)}, u32[]{:S(2)}, u32[]{:S(2)}) collective-permute-start(bf16[256,1024]{1,0:T(8,128)(2,1)} %copy-done.6), channel_id=1, source_target_pairs={{0,24},{8,16},{16,8},{24,0},{1,25},{9,17},{17,9},{25,1},{2,26},{10... | collective-permute-start | bytes 1572872 | tf_op jit(solution)/shard_map/normed_group/ppermute | solution.py:122
  139.1 152.1 %collective-permute-start.11 = (bf16[256,1024]{1,0:T(8,128)(2,1)}, bf16[256,1024]{1,0:T(8,128)(2,1)S(1)}, u32[]{:S(2)}, u32[]{:S(2)}) collective-permute-start(bf16[256,1024]{1,0:T(8,128)(2,1)} %copy-done.6), channel_id=1, source_target_pairs={{0,16},{8,24},{16,0},{24,8},{1,17},{9,25},{17,1},{25,9},{2,18},{10... | collective-permute-start | bytes 1572872 | tf_op jit(solution)/shard_map/normed_group/ppermute | solution.py:122
  158.5 132.7 %collective-permute-start.10 = (bf16[256,1024]{1,0:T(8,128)(2,1)S(1)}, bf16[256,1024]{1,0:T(8,128)(2,1)S(1)}, u32[]{:S(2)}, u32[]{:S(2)}) collective-permute-start(bf16[256,1024]{1,0:T(8,128)(2,1)S(1)} %copy-done.7), channel_id=1, source_target_pairs={{0,8},{8,0},{16,24},{24,16},{1,9},{9,1},{17,25},{25,17},{2,10},{10... | collective-permute-start | bytes 1572872 | tf_op jit(solution)/shard_map/normed_group/ppermute | solution.py:122
  255.5 67.4 %collective-permute-start.21 = (bf16[384,1024]{1,0:T(8,128)(2,1)}, bf16[384,1024]{1,0:T(8,128)(2,1)}, u32[]{:S(2)}, u32[]{:S(2)}) collective-permute-start(bf16[384,1024]{1,0:T(8,128)(2,1)} %convolution_convert_fusion.5), channel_id=1, source_target_pairs={{0,2},{2,0},{4,6},{6,4},{1,3},{3,1},{5,7},{7,5},{8,10},{10,8},{12,... | collective-permute-start | bytes 2359304 | tf_op jit(solution)/shard_map/grad_weight/ppermute | solution.py:122
  258.3 76.8 %collective-permute-start.20 = (bf16[384,1024]{1,0:T(8,128)(2,1)}, bf16[384,1024]{1,0:T(8,128)(2,1)}, u32[]{:S(2)}, u32[]{:S(2)}) collective-permute-start(bf16[384,1024]{1,0:T(8,128)(2,1)} %convolution_convert_fusion.6), channel_id=1, source_target_pairs={{0,4},{2,6},{4,0},{6,2},{1,5},{3,7},{5,1},{7,3},{8,12},{10,14},{12... | collective-permute-start | bytes 2359304 | tf_op jit(solution)/shard_map/grad_weight/ppermute | solution.py:122
  261.9 73.2 %collective-permute-start.19 = (bf16[384,1024]{1,0:T(8,128)(2,1)}, bf16[384,1024]{1,0:T(8,128)(2,1)}, u32[]{:S(2)}, u32[]{:S(2)}) collective-permute-start(bf16[384,1024]{1,0:T(8,128)(2,1)} %convolution_convert_fusion.7), channel_id=1, source_target_pairs={{0,6},{2,4},{4,2},{6,0},{1,7},{3,5},{5,3},{7,1},{8,14},{10,12},{12... | collective-permute-start | bytes 2359304 | tf_op jit(solution)/shard_map/grad_weight/ppermute | solution.py:122
  293.1 45.7 %collective-permute-start.15 = (bf16[384,1024]{1,0:T(8,128)(2,1)}, bf16[384,1024]{1,0:T(8,128)(2,1)}, u32[]{:S(2)}, u32[]{:S(2)}) collective-permute-start(bf16[384,1024]{1,0:T(8,128)(2,1)} %convolution_convert_fusion.9), channel_id=1, source_target_pairs={{0,2},{2,0},{4,6},{6,4},{1,3},{3,1},{5,7},{7,5},{8,10},{10,8},{12,... | collective-permute-start | bytes 2359304 | tf_op jit(solution)/shard_map/grad_weight/ppermute | solution.py:122
  310.0 18.1 %all-to-all-start.2 = ((bf16[16,128,128]{2,1,0:T(8,128)(2,1)}), bf16[16,128,128]{2,1,0:T(8,128)(2,1)}, u32[]{:S(2)}, u32[]{:S(2)}) async-start(bf16[16,128,128]{2,1,0:T(8,128)(2,1)} %copy-done.12), calls=%async_computation.3 | async-start | bytes 1048576 | tf_op jit(solution)/shard_map/back_states/all_to_all | solution.py:179
  318.0 43.2 %collective-permute-start.14 = (bf16[384,1024]{1,0:T(8,128)(2,1)}, bf16[384,1024]{1,0:T(8,128)(2,1)}, u32[]{:S(2)}, u32[]{:S(2)}) collective-permute-start(bf16[384,1024]{1,0:T(8,128)(2,1)} %convolution_convert_fusion.10), channel_id=1, source_target_pairs={{0,4},{2,6},{4,0},{6,2},{1,5},{3,7},{5,1},{7,3},{8,12},{10,14},{12... | collective-permute-start | bytes 2359304 | tf_op jit(solution)/shard_map/grad_weight/ppermute | solution.py:122
  322.8 38.4 %collective-permute-start.13 = (bf16[384,1024]{1,0:T(8,128)(2,1)}, bf16[384,1024]{1,0:T(8,128)(2,1)}, u32[]{:S(2)}, u32[]{:S(2)}) collective-permute-start(bf16[384,1024]{1,0:T(8,128)(2,1)} %convolution_convert_fusion.11), channel_id=1, source_target_pairs={{0,6},{2,4},{4,2},{6,0},{1,7},{3,5},{5,3},{7,1},{8,14},{10,12},{12... | collective-permute-start | bytes 2359304 | tf_op jit(solution)/shard_map/grad_weight/ppermute | solution.py:122
  330.0 36.2 %all-to-all-start.3 = ((bf16[16,128,128]{2,1,0:T(8,128)(2,1)}), bf16[16,128,128]{2,1,0:T(8,128)(2,1)}, u32[]{:S(2)}, u32[]{:S(2)}) async-start(bf16[16,128,128]{2,1,0:T(8,128)(2,1)} %back_states.3), calls=%async_computation.4 | async-start | bytes 1048576 | tf_op jit(solution)/shard_map/back_states/all_to_all | solution.py:194
  (43 other events, 697.9 us)
Sparse Core Ops, SparseCore 0:
  132.5 136.3 reduce-scatter.1

commit v4 on v3

--- a/solution.py
+++ b/solution.py
@@ -240,7 +240,7 @@
             ways = {step: swap(piece, "sa", step) for step in far_first(groups)}
             group.append(jnp.concatenate([piece] + [ways[d] for d in range(1, groups)], axis=0))
     with jax.named_scope("grad_normed"):
-        columns, weight, _ = lax.optimization_barrier((columns, weight, normed))
+        columns, weight, _ = lax.optimization_barrier((columns, weight, scanned))
         weight = jnp.concatenate([weight[d] for d in range(plane)], axis=0)
         partial = [
             jnp.dot(part, weight, preferred_element_type=F32).astype(BF16) for part in columns

time: 391 us -> 445 us (1.14)
  waiting for transfers between devices: 156 us -> 195 us
  matrix products: 28.2 us -> 33.5 us
  starting transfers between devices: 89.6 us -> 94.2 us
    ppermute x22, waiting for transfers between devices: 143 us -> 175 us  [swap(): return lax.ppermute(piece, axis, [(i, i ^ step) for i in range(count)])]
    all_to_all x2, waiting for transfers between devices: 9.4 us -> 18 us  [send_back(): lax.all_to_all(scanned, SEQ, 0, 0, tiled=True).reshape(heads, dim, dim)]
    dot_general x8, matrix products: 21 us -> 26.4 us  [mm(): lax.dot_general(a, b, (((ca,), (cb,)), ((), ())), preferred_element_type=...]
    unnamed x92 -> x86, local copies, waits for them, and re-layouts: 19.4 us -> 17.6 us
  transfers between devices with their start and end apart: 27 -> 27, of which waited for: 9 -> 10; matrix products, arithmetic and copies ran while one was open for 13% -> 14% of each run, Pallas kernels for 10% -> 6%
where the time goes in v4:
time: 445 us; the launch traced here: 440 us
  waiting for transfers between devices  195 us (44%)
  starting transfers between devices  94.2 us (21%)
  Pallas kernels  48.9 us (11%)
  matrix products  33.5 us (8%)
  local copies, waits for them, and re-layouts  32.2 us (7%)
  other arithmetic  21 us (5%)
  between operations  15.6 us (4%)
    ppermute x22, waiting for transfers between devices, swap(): return lax.ppermute(piece, axis, [(i, i ^ step) for i in range(count)])  175 us
    ppermute x22, starting transfers between devices, swap(): return lax.ppermute(piece, axis, [(i, i ^ step) for i in range(count)])  66.7 us
    pallas_call x5, Pallas kernels, per_head(): pl.pallas_call(kernel, grid=(heads,), in_specs=in_specs, out_specs=[kinds...  45 us
    dot_general x8, matrix products, mm(): lax.dot_general(a, b, (((ca,), (cb,)), ((), ())), preferred_element_type=...  26.4 us
    all_to_all x2, waiting for transfers between devices, send_back(): lax.all_to_all(scanned, SEQ, 0, 0, tiled=True).reshape(heads, dim, dim)  18 us
    unnamed x86, local copies, waits for them, and re-layouts  17.6 us
    all_to_all x2, starting transfers between devices, send_back(): lax.all_to_all(scanned, SEQ, 0, 0, tiled=True).reshape(heads, dim, dim)  14.8 us
    all_to_all x2, starting transfers between devices, send_parts(): lax.all_to_all(states.reshape(count, rows, dim), SEQ, 0, 0, tiled=True)  12.6 us
  transfers between devices with their start and end apart: 27, of which 10 were waited for; matrix products, arithmetic and copies ran while one was open for 14% of the time, Pallas kernels for 6%

profile of v4, /device:TPU:0, one launch (start us, length us, event | category | flops | bytes accessed | tf_op | source)
XLA Modules:
  0.0 440.5 jit_solution(4736796327577320415)
XLA Ops:
  16.1 8.5 %states.2 = bf16[16,128,128]{2,1,0:T(8,128)(2,1)} custom-call(f32[16]{0:T(128)S(1)} %copy-done.11, f32[256,4]{1,0:T(8,128)S(1)} %convert_element_type.66.masks, bf16[256,2048]{1,0:T(8,128)(2,1)S(1)} %bitcast.117, bf16[256,2048]{1,0:T(8,128)(2,1)S(1)} %bitcast.122), custom_call_target="tpu_custom_call" | custom-call | flops 134217728 | bytes 3145728 | tf_op jit(solution)/shard_map/states/pallas_call | solution.py:105
  24.6 8.4 %all-to-all-start = ((bf16[16,128,128]{2,1,0:T(8,128)(2,1)}), bf16[16,128,128]{2,1,0:T(8,128)(2,1)}, u32[]{:S(2)}, u32[]{:S(2)}) async-start(bf16[16,128,128]{2,1,0:T(8,128)(2,1)} %states.2), calls=%async_computation | async-start | bytes 1048576 | tf_op jit(solution)/shard_map/states/all_to_all | solution.py:179
  54.9 3.9 collective-permute-done
  58.8 14.9 %collective-permute-done.1 = bf16[128,1536]{1,0:T(8,128)(2,1)} collective-permute-done((bf16[128,1536]{1,0:T(8,128)(2,1)S(1)}, bf16[128,1536]{1,0:T(8,128)(2,1)}, u32[]{:S(2)}, u32[]{:S(2)}) %collective-permute-start.1) | collective-permute-done | bytes 393248 | tf_op jit(solution)/shard_map/grad_columns/ppermute | solution.py:122
  84.3 26.7 %collective-permute-done.7 = bf16[384,2048]{1,0:T(8,128)(2,1)S(1)} collective-permute-done((bf16[384,2048]{1,0:T(8,128)(2,1)S(1)}, bf16[384,2048]{1,0:T(8,128)(2,1)S(1)}, u32[]{:S(2)}, u32[]{:S(2)}) %collective-permute-start.7) | collective-permute-done | bytes 1572896 | tf_op jit(solution)/shard_map/weight_rows/ppermute | solution.py:122
  111.0 34.5 %collective-permute-done.8 = bf16[384,2048]{1,0:T(8,128)(2,1)} collective-permute-done((bf16[384,2048]{1,0:T(8,128)(2,1)S(1)}, bf16[384,2048]{1,0:T(8,128)(2,1)}, u32[]{:S(2)}, u32[]{:S(2)}) %collective-permute-start.8) | collective-permute-done | bytes 1572896 | tf_op jit(solution)/shard_map/weight_rows/ppermute | solution.py:122
  159.6 10.6 %all-to-all-start.1 = ((bf16[16,128,128]{2,1,0:T(8,128)(2,1)}), bf16[16,128,128]{2,1,0:T(8,128)(2,1)}, u32[]{:S(2)}, u32[]{:S(2)}) async-start(bf16[16,128,128]{2,1,0:T(8,128)(2,1)} %states.3), calls=%async_computation.1 | async-start | bytes 1048576 | tf_op jit(solution)/shard_map/states/all_to_all | solution.py:194
  175.8 18.0 %all-to-all-done.1.state = bf16[16,128,128]{2,1,0:T(8,128)(2,1)} async-done(((bf16[16,128,128]{2,1,0:T(8,128)(2,1)}), bf16[16,128,128]{2,1,0:T(8,128)(2,1)}, u32[]{:S(2)}, u32[]{:S(2)}) %all-to-all-start.1) | async-done | bytes 524320 | tf_op jit(solution)/shard_map/states/all_to_all | solution.py:194
  193.8 5.8 %forward.3 = bf16[256,1024]{1,0:T(8,128)(2,1)S(1)} custom-call(f32[8]{0:T(128)S(1)} %get-tuple-element.73.rates, f32[256,4]{1,0:T(8,128)S(1)} %convert_element_type.66.masks, f32[256,256]{1,0:T(8,128)S(1)} %fusion.29.allowed, bf16[256,2048]{1,0:T(8,128)(2,1)S(1)} %bitcast.127, bf16[256,2048]{1,0:T(8,128)(2,1)S(1)} %bitcast.118, ...), custom_call_target="tpu_custom_call" | custom-call | flops 335544320 | bytes 2097152 | tf_op jit(solution)/shard_map/forward/pallas_call | solution.py:105
  199.5 4.1 collective-permute-start.18
  203.7 3.5 collective-permute-start.17
  209.0 5.6 %forward.2 = bf16[256,1024]{1,0:T(8,128)(2,1)S(1)} custom-call(f32[8]{0:T(128)S(1)} %get-tuple-element.72.rates, f32[256,4]{1,0:T(8,128)S(1)} %convert_element_type.66.masks, f32[256,256]{1,0:T(8,128)S(1)} %fusion.29.allowed, bf16[256,2048]{1,0:T(8,128)(2,1)S(1)} %bitcast.128, bf16[256,2048]{1,0:T(8,128)(2,1)S(1)} %bitcast.119, ...), custom_call_target="tpu_custom_call" | custom-call | flops 335544320 | bytes 2097152 | tf_op jit(solution)/shard_map/forward/pallas_call | solution.py:105
  218.2 9.5 %collective-permute-done.18 = bf16[256,1024]{1,0:T(8,128)(2,1)S(1)} collective-permute-done((bf16[256,1024]{1,0:T(8,128)(2,1)S(1)}, bf16[256,1024]{1,0:T(8,128)(2,1)S(1)}, u32[]{:S(2)}, u32[]{:S(2)}) %collective-permute-start.18) | collective-permute-done | bytes 524320 | tf_op jit(solution)/shard_map/normed_group/ppermute | solution.py:122
  227.6 38.6 %collective-permute-start.10 = (bf16[256,1024]{1,0:T(8,128)(2,1)S(1)}, bf16[256,1024]{1,0:T(8,128)(2,1)S(1)}, u32[]{:S(2)}, u32[]{:S(2)}) collective-permute-start(bf16[256,1024]{1,0:T(8,128)(2,1)S(1)} %forward.2), channel_id=1, source_target_pairs={{0,8},{8,0},{16,24},{24,16},{1,9},{9,1},{17,25},{25,17},{2,10},{10... | collective-permute-start | bytes 1572872 | tf_op jit(solution)/shard_map/normed_group/ppermute | solution.py:122
  266.2 50.9 %collective-permute-done.17 = bf16[256,1024]{1,0:T(8,128)(2,1)S(1)} collective-permute-done((bf16[256,1024]{1,0:T(8,128)(2,1)S(1)}, bf16[256,1024]{1,0:T(8,128)(2,1)S(1)}, u32[]{:S(2)}, u32[]{:S(2)}) %collective-permute-start.17) | collective-permute-done | bytes 524320 | tf_op jit(solution)/shard_map/normed_group/ppermute | solution.py:122
  317.2 3.4 convolution_convert_fusion.5
  330.2 11.2 %collective-permute-done.11 = bf16[256,1024]{1,0:T(8,128)(2,1)S(1)} collective-permute-done((bf16[256,1024]{1,0:T(8,128)(2,1)S(1)}, bf16[256,1024]{1,0:T(8,128)(2,1)S(1)}, u32[]{:S(2)}, u32[]{:S(2)}) %collective-permute-start.11) | collective-permute-done | bytes 524320 | tf_op jit(solution)/shard_map/normed_group/ppermute | solution.py:122
  347.6 12.9 %back_states.2 = (bf16[256,2048]{1,0:T(8,128)(2,1)S(1)}, bf16[16,128,128]{2,1,0:T(8,128)(2,1)S(1)}) custom-call(f32[16]{0:T(128)S(1)} %copy-done.12, f32[256,4]{1,0:T(8,128)S(1)} %convert_element_type.66.masks, f32[256,256]{1,0:T(8,128)S(1)} %fusion.29.allowed, bf16[256,2048]{1,0:T(8,128)(2,1)S(1)} %bitcast.129, bf16[256,2048]{1,0:T(8,128)(2,1)S(1)} %bitcast.120, ...), custom_call_target="tpu_custom_call" | custom-call | flops 805306368 | bytes 6291456 | tf_op jit(solution)/shard_map/back_states/pallas_call | solution.py:105
  362.2 4.2 all-to-all-start.2
  366.5 3.8 convolution_convert_fusion.10
  383.4 4.2 all-to-all-start.3
  387.7 3.7 add_multiply_fusion
  391.4 23.7 %collective-permute-done.14 = bf16[384,1024]{1,0:T(8,128)(2,1)} collective-permute-done((bf16[384,1024]{1,0:T(8,128)(2,1)}, bf16[384,1024]{1,0:T(8,128)(2,1)}, u32[]{:S(2)}, u32[]{:S(2)}) %collective-permute-start.14) | collective-permute-done | bytes 786464 | tf_op jit(solution)/shard_map/grad_weight/ppermute | solution.py:122
  421.3 12.3 %grads.1 = (bf16[256,2048]{1,0:T(8,128)(2,1)}, bf16[256,2048]{1,0:T(8,128)(2,1)}, bf16[256,2048]{1,0:T(8,128)(2,1)}) custom-call(f32[16]{0:T(128)S(1)} %copy-done.12, f32[256,4]{1,0:T(8,128)S(1)} %convert_element_type.66.masks, f32[256,256]{1,0:T(8,128)S(1)} %fusion.29.allowed, bf16[256,2048]{1,0:T(8,128)(2,1)S(1)} %bitcast.130, ...), custom_call_target="tpu_custom_call" | custom-call | flops 1744830464 | bytes 7340032 | tf_op jit(solution)/shard_map/grads/pallas_call | solution.py:105
  (196 shorter events, 102.0 us)
Async XLA Ops:
  24.6 28.4 %all-to-all-start = ((bf16[16,128,128]{2,1,0:T(8,128)(2,1)}), bf16[16,128,128]{2,1,0:T(8,128)(2,1)}, u32[]{:S(2)}, u32[]{:S(2)}) async-start(bf16[16,128,128]{2,1,0:T(8,128)(2,1)} %states.2), calls=%async_computation | async-start | bytes 1048576 | tf_op jit(solution)/shard_map/states/all_to_all | solution.py:179
  33.0 313.4 %reduce-scatter.2.cloned.1.call-start = ((), (), s32[]{:S(2)}) async-start(), calls=%async_computation.5 | async-start | bytes 5242880 | tf_op jit(solution)/shard_map/grad_normed/reduce_scatter | solution.py:249
  37.2 21.6 %collective-permute-start = (bf16[128,1536]{1,0:T(8,128)(2,1)S(1)}, bf16[128,1536]{1,0:T(8,128)(2,1)}, u32[]{:S(2)}, u32[]{:S(2)}) collective-permute-start(bf16[128,1536]{1,0:T(8,128)(2,1)S(1)} %pad_maximum_fusion.10), channel_id=1, source_target_pairs={{0,8},{8,0},{16,24},{24,16},{1,9},{9,1},{17,25},{25,17},{2,10},{10... | collective-permute-start | bytes 1179656 | tf_op jit(solution)/shard_map/grad_columns/ppermute | solution.py:122
  42.5 31.2 %collective-permute-start.1 = (bf16[128,1536]{1,0:T(8,128)(2,1)S(1)}, bf16[128,1536]{1,0:T(8,128)(2,1)}, u32[]{:S(2)}, u32[]{:S(2)}) collective-permute-start(bf16[128,1536]{1,0:T(8,128)(2,1)S(1)} %pad_maximum_fusion.11), channel_id=1, source_target_pairs={{0,16},{8,24},{16,0},{24,8},{1,17},{9,25},{17,1},{25,9},{2,18},{10... | collective-permute-start | bytes 1179656 | tf_op jit(solution)/shard_map/grad_columns/ppermute | solution.py:122
  47.7 26.0 %collective-permute-start.2 = (bf16[128,1536]{1,0:T(8,128)(2,1)S(1)}, bf16[128,1536]{1,0:T(8,128)(2,1)}, u32[]{:S(2)}, u32[]{:S(2)}) collective-permute-start(bf16[128,1536]{1,0:T(8,128)(2,1)S(1)} %pad_maximum_fusion.12), channel_id=1, source_target_pairs={{0,24},{8,16},{16,8},{24,0},{1,25},{9,17},{17,9},{25,1},{2,26},{10... | collective-permute-start | bytes 1179656 | tf_op jit(solution)/shard_map/grad_columns/ppermute | solution.py:122
  73.8 37.3 %collective-permute-start.7 = (bf16[384,2048]{1,0:T(8,128)(2,1)S(1)}, bf16[384,2048]{1,0:T(8,128)(2,1)S(1)}, u32[]{:S(2)}, u32[]{:S(2)}) collective-permute-start(bf16[384,2048]{1,0:T(8,128)(2,1)S(1)} %copy-done.22), channel_id=1, source_target_pairs={{0,2},{2,0},{4,6},{6,4},{1,3},{3,1},{5,7},{7,5},{8,10},{10,8},{12,... | collective-permute-start | bytes 4718600 | tf_op jit(solution)/shard_map/weight_rows/ppermute | solution.py:122
  75.3 70.3 %collective-permute-start.8 = (bf16[384,2048]{1,0:T(8,128)(2,1)S(1)}, bf16[384,2048]{1,0:T(8,128)(2,1)}, u32[]{:S(2)}, u32[]{:S(2)}) collective-permute-start(bf16[384,2048]{1,0:T(8,128)(2,1)S(1)} %copy-done.22), channel_id=1, source_target_pairs={{0,4},{2,6},{4,0},{6,2},{1,5},{3,7},{5,1},{7,3},{8,12},{10,14},{12... | collective-permute-start | bytes 4718600 | tf_op jit(solution)/shard_map/weight_rows/ppermute | solution.py:122
  76.8 68.8 %collective-permute-start.9 = (bf16[384,2048]{1,0:T(8,128)(2,1)S(1)}, bf16[384,2048]{1,0:T(8,128)(2,1)}, u32[]{:S(2)}, u32[]{:S(2)}) collective-permute-start(bf16[384,2048]{1,0:T(8,128)(2,1)S(1)} %copy-done.22), channel_id=1, source_target_pairs={{0,6},{2,4},{4,2},{6,0},{1,7},{3,5},{5,3},{7,1},{8,14},{10,12},{12... | collective-permute-start | bytes 4718600 | tf_op jit(solution)/shard_map/weight_rows/ppermute | solution.py:122
  77.3 3.6 collective-permute-start.5
  159.6 34.2 %all-to-all-start.1 = ((bf16[16,128,128]{2,1,0:T(8,128)(2,1)}), bf16[16,128,128]{2,1,0:T(8,128)(2,1)}, u32[]{:S(2)}, u32[]{:S(2)}) async-start(bf16[16,128,128]{2,1,0:T(8,128)(2,1)} %states.3), calls=%async_computation.1 | async-start | bytes 1048576 | tf_op jit(solution)/shard_map/states/all_to_all | solution.py:194
  199.5 28.1 %collective-permute-start.18 = (bf16[256,1024]{1,0:T(8,128)(2,1)S(1)}, bf16[256,1024]{1,0:T(8,128)(2,1)S(1)}, u32[]{:S(2)}, u32[]{:S(2)}) collective-permute-start(bf16[256,1024]{1,0:T(8,128)(2,1)S(1)} %forward.3), channel_id=1, source_target_pairs={{0,24},{8,16},{16,8},{24,0},{1,25},{9,17},{17,9},{25,1},{2,26},{10... | collective-permute-start | bytes 1572872 | tf_op jit(solution)/shard_map/normed_group/ppermute | solution.py:122
  203.7 113.5 %collective-permute-start.17 = (bf16[256,1024]{1,0:T(8,128)(2,1)S(1)}, bf16[256,1024]{1,0:T(8,128)(2,1)S(1)}, u32[]{:S(2)}, u32[]{:S(2)}) collective-permute-start(bf16[256,1024]{1,0:T(8,128)(2,1)S(1)} %forward.3), channel_id=1, source_target_pairs={{0,16},{8,24},{16,0},{24,8},{1,17},{9,25},{17,1},{25,9},{2,18},{10... | collective-permute-start | bytes 1572872 | tf_op jit(solution)/shard_map/normed_group/ppermute | solution.py:122
  207.1 110.0 %collective-permute-start.16 = (bf16[256,1024]{1,0:T(8,128)(2,1)S(1)}, bf16[256,1024]{1,0:T(8,128)(2,1)S(1)}, u32[]{:S(2)}, u32[]{:S(2)}) collective-permute-start(bf16[256,1024]{1,0:T(8,128)(2,1)S(1)} %forward.3), channel_id=1, source_target_pairs={{0,8},{8,0},{16,24},{24,16},{1,9},{9,1},{17,25},{25,17},{2,10},{10... | collective-permute-start | bytes 1572872 | tf_op jit(solution)/shard_map/normed_group/ppermute | solution.py:122
  214.6 115.0 %collective-permute-start.12 = (bf16[256,1024]{1,0:T(8,128)(2,1)S(1)}, bf16[256,1024]{1,0:T(8,128)(2,1)S(1)}, u32[]{:S(2)}, u32[]{:S(2)}) collective-permute-start(bf16[256,1024]{1,0:T(8,128)(2,1)S(1)} %forward.2), channel_id=1, source_target_pairs={{0,24},{8,16},{16,8},{24,0},{1,25},{9,17},{17,9},{25,1},{2,26},{10... | collective-permute-start | bytes 1572872 | tf_op jit(solution)/shard_map/normed_group/ppermute | solution.py:122
  216.9 124.5 %collective-permute-start.11 = (bf16[256,1024]{1,0:T(8,128)(2,1)S(1)}, bf16[256,1024]{1,0:T(8,128)(2,1)S(1)}, u32[]{:S(2)}, u32[]{:S(2)}) collective-permute-start(bf16[256,1024]{1,0:T(8,128)(2,1)S(1)} %forward.2), channel_id=1, source_target_pairs={{0,16},{8,24},{16,0},{24,8},{1,17},{9,25},{17,1},{25,9},{2,18},{10... | collective-permute-start | bytes 1572872 | tf_op jit(solution)/shard_map/normed_group/ppermute | solution.py:122
  227.6 113.8 %collective-permute-start.10 = (bf16[256,1024]{1,0:T(8,128)(2,1)S(1)}, bf16[256,1024]{1,0:T(8,128)(2,1)S(1)}, u32[]{:S(2)}, u32[]{:S(2)}) collective-permute-start(bf16[256,1024]{1,0:T(8,128)(2,1)S(1)} %forward.2), channel_id=1, source_target_pairs={{0,8},{8,0},{16,24},{24,16},{1,9},{9,1},{17,25},{25,17},{2,10},{10... | collective-permute-start | bytes 1572872 | tf_op jit(solution)/shard_map/normed_group/ppermute | solution.py:122
  320.6 54.6 %collective-permute-start.21 = (bf16[384,1024]{1,0:T(8,128)(2,1)}, bf16[384,1024]{1,0:T(8,128)(2,1)}, u32[]{:S(2)}, u32[]{:S(2)}) collective-permute-start(bf16[384,1024]{1,0:T(8,128)(2,1)} %convolution_convert_fusion.5), channel_id=1, source_target_pairs={{0,2},{2,0},{4,6},{6,4},{1,3},{3,1},{5,7},{7,5},{8,10},{10,8},{12,... | collective-permute-start | bytes 2359304 | tf_op jit(solution)/shard_map/grad_weight/ppermute | solution.py:122
  325.1 62.6 %collective-permute-start.20 = (bf16[384,1024]{1,0:T(8,128)(2,1)}, bf16[384,1024]{1,0:T(8,128)(2,1)}, u32[]{:S(2)}, u32[]{:S(2)}) collective-permute-start(bf16[384,1024]{1,0:T(8,128)(2,1)} %convolution_convert_fusion.6), channel_id=1, source_target_pairs={{0,4},{2,6},{4,0},{6,2},{1,5},{3,7},{5,1},{7,3},{8,12},{10,14},{12... | collective-permute-start | bytes 2359304 | tf_op jit(solution)/shard_map/grad_weight/ppermute | solution.py:122
  329.7 58.0 %collective-permute-start.19 = (bf16[384,1024]{1,0:T(8,128)(2,1)}, bf16[384,1024]{1,0:T(8,128)(2,1)}, u32[]{:S(2)}, u32[]{:S(2)}) collective-permute-start(bf16[384,1024]{1,0:T(8,128)(2,1)} %convolution_convert_fusion.7), channel_id=1, source_target_pairs={{0,6},{2,4},{4,2},{6,0},{1,7},{3,5},{5,3},{7,1},{8,14},{10,12},{12... | collective-permute-start | bytes 2359304 | tf_op jit(solution)/shard_map/grad_weight/ppermute | solution.py:122
  344.8 46.6 %collective-permute-start.15 = (bf16[384,1024]{1,0:T(8,128)(2,1)}, bf16[384,1024]{1,0:T(8,128)(2,1)}, u32[]{:S(2)}, u32[]{:S(2)}) collective-permute-start(bf16[384,1024]{1,0:T(8,128)(2,1)} %convolution_convert_fusion.9), channel_id=1, source_target_pairs={{0,2},{2,0},{4,6},{6,4},{1,3},{3,1},{5,7},{7,5},{8,10},{10,8},{12,... | collective-permute-start | bytes 2359304 | tf_op jit(solution)/shard_map/grad_weight/ppermute | solution.py:122
  362.2 19.2 %all-to-all-start.2 = ((bf16[16,128,128]{2,1,0:T(8,128)(2,1)}), bf16[16,128,128]{2,1,0:T(8,128)(2,1)}, u32[]{:S(2)}, u32[]{:S(2)}) async-start(bf16[16,128,128]{2,1,0:T(8,128)(2,1)} %copy-done.10), calls=%async_computation.3 | async-start | bytes 1048576 | tf_op jit(solution)/shard_map/back_states/all_to_all | solution.py:179
  370.3 44.8 %collective-permute-start.14 = (bf16[384,1024]{1,0:T(8,128)(2,1)}, bf16[384,1024]{1,0:T(8,128)(2,1)}, u32[]{:S(2)}, u32[]{:S(2)}) collective-permute-start(bf16[384,1024]{1,0:T(8,128)(2,1)} %convolution_convert_fusion.10), channel_id=1, source_target_pairs={{0,4},{2,6},{4,0},{6,2},{1,5},{3,7},{5,1},{7,3},{8,12},{10,14},{12... | collective-permute-start | bytes 2359304 | tf_op jit(solution)/shard_map/grad_weight/ppermute | solution.py:122
  375.2 40.0 %collective-permute-start.13 = (bf16[384,1024]{1,0:T(8,128)(2,1)}, bf16[384,1024]{1,0:T(8,128)(2,1)}, u32[]{:S(2)}, u32[]{:S(2)}) collective-permute-start(bf16[384,1024]{1,0:T(8,128)(2,1)} %convolution_convert_fusion.11), channel_id=1, source_target_pairs={{0,6},{2,4},{4,2},{6,0},{1,7},{3,5},{5,3},{7,1},{8,14},{10,12},{12... | collective-permute-start | bytes 2359304 | tf_op jit(solution)/shard_map/grad_weight/ppermute | solution.py:122
  383.4 36.7 %all-to-all-start.3 = ((bf16[16,128,128]{2,1,0:T(8,128)(2,1)}), bf16[16,128,128]{2,1,0:T(8,128)(2,1)}, u32[]{:S(2)}, u32[]{:S(2)}) async-start(bf16[16,128,128]{2,1,0:T(8,128)(2,1)} %back_states.3), calls=%async_computation.4 | async-start | bytes 1048576 | tf_op jit(solution)/shard_map/back_states/all_to_all | solution.py:194
  (40 other events, 1018.2 us)
Sparse Core Ops, SparseCore 0:
  159.6 139.5 reduce-scatter.1

commit v5 on v3

--- a/solution.py
+++ b/solution.py
@@ -236,8 +236,11 @@
             )
     with jax.named_scope("normed_group"):
         group = []
+        arrived = ()
         for piece in normed:
+            piece, _ = lax.optimization_barrier((piece, arrived))
             ways = {step: swap(piece, "sa", step) for step in far_first(groups)}
+            arrived = tuple(ways.values())
             group.append(jnp.concatenate([piece] + [ways[d] for d in range(1, groups)], axis=0))
     with jax.named_scope("grad_normed"):
         columns, weight, _ = lax.optimization_barrier((columns, weight, normed))

time: 391 us -> 391 us (level)
  starting transfers between devices: 89.6 us -> 64.9 us
  waiting for transfers between devices: 156 us -> 174 us
    ppermute x22, starting transfers between devices: 64 us -> 30 us  [swap(): return lax.ppermute(piece, axis, [(i, i ^ step) for i in range(count)])]
    ppermute x22, waiting for transfers between devices: 143 us -> 162 us  [swap(): return lax.ppermute(piece, axis, [(i, i ^ step) for i in range(count)])]
    all_to_all x2, starting transfers between devices: 9.27 us -> 16.8 us  [send_parts(): lax.all_to_all(states.reshape(count, rows, dim), SEQ, 0, 0, tiled=True)]
    unnamed x92 -> x75, local copies, waits for them, and re-layouts: 19.4 us -> 22.2 us
  transfers between devices with their start and end apart: 27 -> 27, of which waited for: 9 -> 11; matrix products, arithmetic and copies ran while one was open for 13% -> 15% of each run, Pallas kernels for 10% -> 10%
where the time goes in v5:
time: 391 us; the launch traced here: 387 us
  waiting for transfers between devices  174 us (45%)
  starting transfers between devices  64.9 us (17%)
  Pallas kernels  49 us (13%)
  local copies, waits for them, and re-layouts  33.4 us (9%)
  matrix products  30.9 us (8%)
  other arithmetic  18.4 us (5%)
  between operations  15.5 us (4%)
    ppermute x22, waiting for transfers between devices, swap(): return lax.ppermute(piece, axis, [(i, i ^ step) for i in range(count)])  162 us
    pallas_call x5, Pallas kernels, per_head(): pl.pallas_call(kernel, grid=(heads,), in_specs=in_specs, out_specs=[kinds...  45.1 us
    ppermute x22, starting transfers between devices, swap(): return lax.ppermute(piece, axis, [(i, i ^ step) for i in range(count)])  30 us
    dot_general x8, matrix products, mm(): lax.dot_general(a, b, (((ca,), (cb,)), ((), ())), preferred_element_type=...  23.7 us
    unnamed x75, local copies, waits for them, and re-layouts  22.2 us
    all_to_all x2, starting transfers between devices, send_back(): lax.all_to_all(scanned, SEQ, 0, 0, tiled=True).reshape(heads, dim, dim)  18.2 us
    all_to_all x2, starting transfers between devices, send_parts(): lax.all_to_all(states.reshape(count, rows, dim), SEQ, 0, 0, tiled=True)  16.8 us
    all_to_all x2, waiting for transfers between devices, send_back(): lax.all_to_all(scanned, SEQ, 0, 0, tiled=True).reshape(heads, dim, dim)  9.4 us
  transfers between devices with their start and end apart: 27, of which 11 were waited for; matrix products, arithmetic and copies ran while one was open for 15% of the time, Pallas kernels for 10%

profile of v5, /device:TPU:0, one launch (start us, length us, event | category | flops | bytes accessed | tf_op | source)
XLA Modules:
  0.0 386.5 jit_solution(18186003604612556153)
XLA Ops:
  20.6 8.5 %states.2 = bf16[16,128,128]{2,1,0:T(8,128)(2,1)} custom-call(f32[16]{0:T(128)S(1)} %copy-done.11, f32[256,4]{1,0:T(8,128)S(1)} %convert_element_type.66.masks, bf16[256,2048]{1,0:T(8,128)(2,1)S(1)} %bitcast.121, bf16[256,2048]{1,0:T(8,128)(2,1)S(1)} %bitcast.126), custom_call_target="tpu_custom_call" | custom-call | flops 134217728 | bytes 3145728 | tf_op jit(solution)/shard_map/states/pallas_call | solution.py:105
  29.1 5.0 %all-to-all-start = ((bf16[16,128,128]{2,1,0:T(8,128)(2,1)}), bf16[16,128,128]{2,1,0:T(8,128)(2,1)}, u32[]{:S(2)}, u32[]{:S(2)}) async-start(bf16[16,128,128]{2,1,0:T(8,128)(2,1)} %states.2), calls=%async_computation | async-start | bytes 1048576 | tf_op jit(solution)/shard_map/states/all_to_all | solution.py:179
  53.9 5.4 %collective-permute-done = bf16[128,1536]{1,0:T(8,128)(2,1)S(1)} collective-permute-done((bf16[128,1536]{1,0:T(8,128)(2,1)S(1)}, bf16[128,1536]{1,0:T(8,128)(2,1)S(1)}, u32[]{:S(2)}, u32[]{:S(2)}) %collective-permute-start) | collective-permute-done | bytes 393248 | tf_op jit(solution)/shard_map/grad_columns/ppermute | solution.py:122
  61.7 12.6 %collective-permute-done.1 = bf16[128,1536]{1,0:T(8,128)(2,1)S(1)} collective-permute-done((bf16[128,1536]{1,0:T(8,128)(2,1)S(1)}, bf16[128,1536]{1,0:T(8,128)(2,1)S(1)}, u32[]{:S(2)}, u32[]{:S(2)}) %collective-permute-start.1) | collective-permute-done | bytes 393248 | tf_op jit(solution)/shard_map/grad_columns/ppermute | solution.py:122
  74.4 11.3 %all-to-all-start.1 = ((bf16[16,128,128]{2,1,0:T(8,128)(2,1)}), bf16[16,128,128]{2,1,0:T(8,128)(2,1)}, u32[]{:S(2)}, u32[]{:S(2)}) async-start(bf16[16,128,128]{2,1,0:T(8,128)(2,1)} %states.3), calls=%async_computation.1 | async-start | bytes 1048576 | tf_op jit(solution)/shard_map/states/all_to_all | solution.py:194
  93.6 9.4 %all-to-all-done.1.state = bf16[16,128,128]{2,1,0:T(8,128)(2,1)} async-done(((bf16[16,128,128]{2,1,0:T(8,128)(2,1)}), bf16[16,128,128]{2,1,0:T(8,128)(2,1)}, u32[]{:S(2)}, u32[]{:S(2)}) %all-to-all-start.1) | async-done | bytes 524320 | tf_op jit(solution)/shard_map/states/all_to_all | solution.py:194
  103.1 5.8 %forward.2 = bf16[256,1024]{1,0:T(8,128)(2,1)S(1)} custom-call(f32[8]{0:T(128)S(1)} %get-tuple-element.75.rates, f32[256,4]{1,0:T(8,128)S(1)} %convert_element_type.66.masks, f32[256,256]{1,0:T(8,128)S(1)} %fusion.29.allowed, bf16[256,2048]{1,0:T(8,128)(2,1)S(1)} %bitcast.131, bf16[256,2048]{1,0:T(8,128)(2,1)S(1)} %bitcast.122, ...), custom_call_target="tpu_custom_call" | custom-call | flops 335544320 | bytes 2097152 | tf_op jit(solution)/shard_map/forward/pallas_call | solution.py:105
  109.7 5.6 %forward.3 = bf16[256,1024]{1,0:T(8,128)(2,1)S(1)} custom-call(f32[8]{0:T(128)S(1)} %get-tuple-element.74.rates, f32[256,4]{1,0:T(8,128)S(1)} %convert_element_type.66.masks, f32[256,256]{1,0:T(8,128)S(1)} %fusion.29.allowed, bf16[256,2048]{1,0:T(8,128)(2,1)S(1)} %bitcast.132, bf16[256,2048]{1,0:T(8,128)(2,1)S(1)} %bitcast.123, ...), custom_call_target="tpu_custom_call" | custom-call | flops 335544320 | bytes 2097152 | tf_op jit(solution)/shard_map/forward/pallas_call | solution.py:105
  140.3 18.2 %collective-permute-done.12 = bf16[256,1024]{1,0:T(8,128)(2,1)S(1)} collective-permute-done((bf16[256,1024]{1,0:T(8,128)(2,1)}, bf16[256,1024]{1,0:T(8,128)(2,1)S(1)}, u32[]{:S(2)}, u32[]{:S(2)}) %collective-permute-start.12) | collective-permute-done | bytes 524320 | tf_op jit(solution)/shard_map/normed_group/ppermute | solution.py:122
  158.5 76.3 %collective-permute-done.11 = bf16[256,1024]{1,0:T(8,128)(2,1)S(1)} collective-permute-done((bf16[256,1024]{1,0:T(8,128)(2,1)}, bf16[256,1024]{1,0:T(8,128)(2,1)S(1)}, u32[]{:S(2)}, u32[]{:S(2)}) %collective-permute-start.11) | collective-permute-done | bytes 524320 | tf_op jit(solution)/shard_map/normed_group/ppermute | solution.py:122
  235.0 4.3 %collective-permute-start.18 = (bf16[256,1024]{1,0:T(8,128)(2,1)S(1)}, bf16[256,1024]{1,0:T(8,128)(2,1)S(1)}, u32[]{:S(2)}, u32[]{:S(2)}) collective-permute-start(bf16[256,1024]{1,0:T(8,128)(2,1)S(1)} %copy-done.6), channel_id=1, source_target_pairs={{0,24},{8,16},{16,8},{24,0},{1,25},{9,17},{17,9},{25,1},{2,26},{10... | collective-permute-start | bytes 1572872 | tf_op jit(solution)/shard_map/normed_group/ppermute | solution.py:122
  247.0 9.3 %collective-permute-done.16 = bf16[256,1024]{1,0:T(8,128)(2,1)S(1)} collective-permute-done((bf16[256,1024]{1,0:T(8,128)(2,1)S(1)}, bf16[256,1024]{1,0:T(8,128)(2,1)S(1)}, u32[]{:S(2)}, u32[]{:S(2)}) %collective-permute-start.16) | collective-permute-done | bytes 524320 | tf_op jit(solution)/shard_map/normed_group/ppermute | solution.py:122
  256.4 4.2 %collective-permute-start.13 = (bf16[384,1024]{1,0:T(8,128)(2,1)}, bf16[384,1024]{1,0:T(8,128)(2,1)}, u32[]{:S(2)}, u32[]{:S(2)}) collective-permute-start(bf16[384,1024]{1,0:T(8,128)(2,1)} %convolution_convert_fusion.11), channel_id=1, source_target_pairs={{0,6},{2,4},{4,2},{6,0},{1,7},{3,5},{5,3},{7,1},{8,14},{10,12},{12... | collective-permute-start | bytes 2359304 | tf_op jit(solution)/shard_map/grad_weight/ppermute | solution.py:122
  261.4 20.8 %collective-permute-done.17 = bf16[256,1024]{1,0:T(8,128)(2,1)S(1)} collective-permute-done((bf16[256,1024]{1,0:T(8,128)(2,1)S(1)}, bf16[256,1024]{1,0:T(8,128)(2,1)S(1)}, u32[]{:S(2)}, u32[]{:S(2)}) %collective-permute-start.17) | collective-permute-done | bytes 524320 | tf_op jit(solution)/shard_map/normed_group/ppermute | solution.py:122
  285.1 12.9 %back_states.2 = (bf16[256,2048]{1,0:T(8,128)(2,1)S(1)}, bf16[16,128,128]{2,1,0:T(8,128)(2,1)S(1)}) custom-call(f32[16]{0:T(128)S(1)} %copy-done.12, f32[256,4]{1,0:T(8,128)S(1)} %convert_element_type.66.masks, f32[256,256]{1,0:T(8,128)S(1)} %fusion.29.allowed, bf16[256,2048]{1,0:T(8,128)(2,1)S(1)} %bitcast.133, bf16[256,2048]{1,0:T(8,128)(2,1)S(1)} %bitcast.124, ...), custom_call_target="tpu_custom_call" | custom-call | flops 805306368 | bytes 6291456 | tf_op jit(solution)/shard_map/back_states/pallas_call | solution.py:105
  299.7 11.7 %all-to-all-start.2 = ((bf16[16,128,128]{2,1,0:T(8,128)(2,1)}), bf16[16,128,128]{2,1,0:T(8,128)(2,1)}, u32[]{:S(2)}, u32[]{:S(2)}) async-start(bf16[16,128,128]{2,1,0:T(8,128)(2,1)} %copy-done.10), calls=%async_computation.3 | async-start | bytes 1048576 | tf_op jit(solution)/shard_map/back_states/all_to_all | solution.py:179
  311.5 3.9 %convolution_convert_fusion.5 = bf16[384,1024]{1,0:T(8,128)(2,1)} fusion(bf16[1024,1024]{1,0:T(8,128)(2,1)} %constant_dynamic-update-slice_fusion.8, bf16[1024,1536]{1,0:T(8,128)(2,1)} %copy-done.16), kind=kOutput, calls=%fused_computation.19 | convolution fusion | flops 805699584 | bytes 3670016 | tf_op jit(solution)/shard_map/grad_weight/dot_general | solution.py:18
  322.2 3.5 convolution_convert_fusion.7
  331.0 6.9 %all-to-all-start.3 = ((bf16[16,128,128]{2,1,0:T(8,128)(2,1)}), bf16[16,128,128]{2,1,0:T(8,128)(2,1)}, u32[]{:S(2)}, u32[]{:S(2)}) async-start(bf16[16,128,128]{2,1,0:T(8,128)(2,1)} %back_states.3), calls=%async_computation.4 | async-start | bytes 1048576 | tf_op jit(solution)/shard_map/back_states/all_to_all | solution.py:194
  338.0 3.6 add_multiply_fusion.1
  342.1 4.1 %collective-permute-done.20 = bf16[384,1024]{1,0:T(8,128)(2,1)} collective-permute-done((bf16[384,1024]{1,0:T(8,128)(2,1)}, bf16[384,1024]{1,0:T(8,128)(2,1)}, u32[]{:S(2)}, u32[]{:S(2)}) %collective-permute-start.20) | collective-permute-done | bytes 786464 | tf_op jit(solution)/shard_map/grad_weight/ppermute | solution.py:122
  346.2 14.4 %collective-permute-done.19 = bf16[384,1024]{1,0:T(8,128)(2,1)} collective-permute-done((bf16[384,1024]{1,0:T(8,128)(2,1)}, bf16[384,1024]{1,0:T(8,128)(2,1)}, u32[]{:S(2)}, u32[]{:S(2)}) %collective-permute-start.19) | collective-permute-done | bytes 786464 | tf_op jit(solution)/shard_map/grad_weight/ppermute | solution.py:122
  360.6 3.6 add_multiply_fusion
  367.4 12.3 %grads.1 = (bf16[256,2048]{1,0:T(8,128)(2,1)}, bf16[256,2048]{1,0:T(8,128)(2,1)}, bf16[256,2048]{1,0:T(8,128)(2,1)}) custom-call(f32[16]{0:T(128)S(1)} %copy-done.12, f32[256,4]{1,0:T(8,128)S(1)} %convert_element_type.66.masks, f32[256,256]{1,0:T(8,128)S(1)} %fusion.29.allowed, bf16[256,2048]{1,0:T(8,128)(2,1)S(1)} %bitcast.134, ...), custom_call_target="tpu_custom_call" | custom-call | flops 1744830464 | bytes 7340032 | tf_op jit(solution)/shard_map/grads/pallas_call | solution.py:105
  (186 shorter events, 97.4 us)
Async XLA Ops:
  7.2 108.2 %collective-permute-start.7 = (bf16[384,2048]{1,0:T(8,128)(2,1)}, bf16[384,2048]{1,0:T(8,128)(2,1)}, u32[]{:S(2)}, u32[]{:S(2)}) collective-permute-start(bf16[384,2048]{1,0:T(8,128)(2,1)} %param.11), channel_id=1, source_target_pairs={{0,2},{2,0},{4,6},{6,4},{1,3},{3,1},{5,7},{7,5},{8,10},{10,8},{12,... | collective-permute-start | bytes 4718600 | tf_op jit(solution)/shard_map/weight_rows/ppermute | solution.py:122
  10.2 105.2 %collective-permute-start.8 = (bf16[384,2048]{1,0:T(8,128)(2,1)}, bf16[384,2048]{1,0:T(8,128)(2,1)}, u32[]{:S(2)}, u32[]{:S(2)}) collective-permute-start(bf16[384,2048]{1,0:T(8,128)(2,1)} %param.11), channel_id=1, source_target_pairs={{0,4},{2,6},{4,0},{6,2},{1,5},{3,7},{5,1},{7,3},{8,12},{10,14},{12... | collective-permute-start | bytes 4718600 | tf_op jit(solution)/shard_map/weight_rows/ppermute | solution.py:122
  29.1 22.9 %all-to-all-start = ((bf16[16,128,128]{2,1,0:T(8,128)(2,1)}), bf16[16,128,128]{2,1,0:T(8,128)(2,1)}, u32[]{:S(2)}, u32[]{:S(2)}) async-start(bf16[16,128,128]{2,1,0:T(8,128)(2,1)} %states.2), calls=%async_computation | async-start | bytes 1048576 | tf_op jit(solution)/shard_map/states/all_to_all | solution.py:179
  38.3 21.0 %collective-permute-start = (bf16[128,1536]{1,0:T(8,128)(2,1)S(1)}, bf16[128,1536]{1,0:T(8,128)(2,1)S(1)}, u32[]{:S(2)}, u32[]{:S(2)}) collective-permute-start(bf16[128,1536]{1,0:T(8,128)(2,1)S(1)} %pad_maximum_fusion.9), channel_id=1, source_target_pairs={{0,8},{8,0},{16,24},{24,16},{1,9},{9,1},{17,25},{25,17},{2,10},{10... | collective-permute-start | bytes 1179656 | tf_op jit(solution)/shard_map/grad_columns/ppermute | solution.py:122
  40.7 33.5 %collective-permute-start.1 = (bf16[128,1536]{1,0:T(8,128)(2,1)S(1)}, bf16[128,1536]{1,0:T(8,128)(2,1)S(1)}, u32[]{:S(2)}, u32[]{:S(2)}) collective-permute-start(bf16[128,1536]{1,0:T(8,128)(2,1)S(1)} %pad_maximum_fusion.10), channel_id=1, source_target_pairs={{0,16},{8,24},{16,0},{24,8},{1,17},{9,25},{17,1},{25,9},{2,18},{10... | collective-permute-start | bytes 1179656 | tf_op jit(solution)/shard_map/grad_columns/ppermute | solution.py:122
  43.7 30.5 %collective-permute-start.2 = (bf16[128,1536]{1,0:T(8,128)(2,1)S(1)}, bf16[128,1536]{1,0:T(8,128)(2,1)}, u32[]{:S(2)}, u32[]{:S(2)}) collective-permute-start(bf16[128,1536]{1,0:T(8,128)(2,1)S(1)} %pad_maximum_fusion.11), channel_id=1, source_target_pairs={{0,24},{8,16},{16,8},{24,0},{1,25},{9,17},{17,9},{25,1},{2,26},{10... | collective-permute-start | bytes 1179656 | tf_op jit(solution)/shard_map/grad_columns/ppermute | solution.py:122
  59.3 56.0 %collective-permute-start.9 = (bf16[384,2048]{1,0:T(8,128)(2,1)}, bf16[384,2048]{1,0:T(8,128)(2,1)}, u32[]{:S(2)}, u32[]{:S(2)}) collective-permute-start(bf16[384,2048]{1,0:T(8,128)(2,1)} %param.11), channel_id=1, source_target_pairs={{0,6},{2,4},{4,2},{6,0},{1,7},{3,5},{5,3},{7,1},{8,14},{10,12},{12... | collective-permute-start | bytes 4718600 | tf_op jit(solution)/shard_map/weight_rows/ppermute | solution.py:122
  74.3 11.8 %collective-permute-start.3 = (bf16[128,1536]{1,0:T(8,128)(2,1)S(1)}, bf16[128,1536]{1,0:T(8,128)(2,1)S(1)}, u32[]{:S(2)}, u32[]{:S(2)}) collective-permute-start(bf16[128,1536]{1,0:T(8,128)(2,1)S(1)} %pad_maximum_fusion.8), channel_id=1, source_target_pairs={{0,1},{1,0},{2,3},{3,2},{4,5},{5,4},{6,7},{7,6},{8,9},{9,8},{10,11... | collective-permute-start | bytes 1179656 | tf_op jit(solution)/shard_map/grad_columns/ppermute | solution.py:122
  74.4 28.6 %all-to-all-start.1 = ((bf16[16,128,128]{2,1,0:T(8,128)(2,1)}), bf16[16,128,128]{2,1,0:T(8,128)(2,1)}, u32[]{:S(2)}, u32[]{:S(2)}) async-start(bf16[16,128,128]{2,1,0:T(8,128)(2,1)} %states.3), calls=%async_computation.1 | async-start | bytes 1048576 | tf_op jit(solution)/shard_map/states/all_to_all | solution.py:194
  85.7 198.1 %reduce-scatter.2.cloned.1.call-start = ((), (), s32[]{:S(2)}) async-start(), calls=%async_computation.5 | async-start | bytes 5242880 | tf_op jit(solution)/shard_map/grad_normed/reduce_scatter | solution.py:252
  133.1 25.4 %collective-permute-start.12 = (bf16[256,1024]{1,0:T(8,128)(2,1)}, bf16[256,1024]{1,0:T(8,128)(2,1)S(1)}, u32[]{:S(2)}, u32[]{:S(2)}) collective-permute-start(bf16[256,1024]{1,0:T(8,128)(2,1)} %copy-done.8), channel_id=1, source_target_pairs={{0,24},{8,16},{16,8},{24,0},{1,25},{9,17},{17,9},{25,1},{2,26},{10... | collective-permute-start | bytes 1572872 | tf_op jit(solution)/shard_map/normed_group/ppermute | solution.py:122
  134.8 100.1 %collective-permute-start.11 = (bf16[256,1024]{1,0:T(8,128)(2,1)}, bf16[256,1024]{1,0:T(8,128)(2,1)S(1)}, u32[]{:S(2)}, u32[]{:S(2)}) collective-permute-start(bf16[256,1024]{1,0:T(8,128)(2,1)} %copy-done.8), channel_id=1, source_target_pairs={{0,16},{8,24},{16,0},{24,8},{1,17},{9,25},{17,1},{25,9},{2,18},{10... | collective-permute-start | bytes 1572872 | tf_op jit(solution)/shard_map/normed_group/ppermute | solution.py:122
  134.8 100.1 %collective-permute-start.10 = (bf16[256,1024]{1,0:T(8,128)(2,1)}, bf16[256,1024]{1,0:T(8,128)(2,1)S(1)}, u32[]{:S(2)}, u32[]{:S(2)}) collective-permute-start(bf16[256,1024]{1,0:T(8,128)(2,1)} %copy-done.8), channel_id=1, source_target_pairs={{0,8},{8,0},{16,24},{24,16},{1,9},{9,1},{17,25},{25,17},{2,10},{10... | collective-permute-start | bytes 1572872 | tf_op jit(solution)/shard_map/normed_group/ppermute | solution.py:122
  234.9 21.5 %collective-permute-start.16 = (bf16[256,1024]{1,0:T(8,128)(2,1)S(1)}, bf16[256,1024]{1,0:T(8,128)(2,1)S(1)}, u32[]{:S(2)}, u32[]{:S(2)}) collective-permute-start(bf16[256,1024]{1,0:T(8,128)(2,1)S(1)} %copy-done.6), channel_id=1, source_target_pairs={{0,8},{8,0},{16,24},{24,16},{1,9},{9,1},{17,25},{25,17},{2,10},{10... | collective-permute-start | bytes 1572872 | tf_op jit(solution)/shard_map/normed_group/ppermute | solution.py:122
  234.9 47.3 %collective-permute-start.17 = (bf16[256,1024]{1,0:T(8,128)(2,1)S(1)}, bf16[256,1024]{1,0:T(8,128)(2,1)S(1)}, u32[]{:S(2)}, u32[]{:S(2)}) collective-permute-start(bf16[256,1024]{1,0:T(8,128)(2,1)S(1)} %copy-done.6), channel_id=1, source_target_pairs={{0,16},{8,24},{16,0},{24,8},{1,17},{9,25},{17,1},{25,9},{2,18},{10... | collective-permute-start | bytes 1572872 | tf_op jit(solution)/shard_map/normed_group/ppermute | solution.py:122
  235.0 48.0 %collective-permute-start.18 = (bf16[256,1024]{1,0:T(8,128)(2,1)S(1)}, bf16[256,1024]{1,0:T(8,128)(2,1)S(1)}, u32[]{:S(2)}, u32[]{:S(2)}) collective-permute-start(bf16[256,1024]{1,0:T(8,128)(2,1)S(1)} %copy-done.6), channel_id=1, source_target_pairs={{0,24},{8,16},{16,8},{24,0},{1,25},{9,17},{17,9},{25,1},{2,26},{10... | collective-permute-start | bytes 1572872 | tf_op jit(solution)/shard_map/normed_group/ppermute | solution.py:122
  241.2 84.5 %collective-permute-start.15 = (bf16[384,1024]{1,0:T(8,128)(2,1)}, bf16[384,1024]{1,0:T(8,128)(2,1)}, u32[]{:S(2)}, u32[]{:S(2)}) collective-permute-start(bf16[384,1024]{1,0:T(8,128)(2,1)} %convolution_convert_fusion.9), channel_id=1, source_target_pairs={{0,2},{2,0},{4,6},{6,4},{1,3},{3,1},{5,7},{7,5},{8,10},{10,8},{12,... | collective-permute-start | bytes 2359304 | tf_op jit(solution)/shard_map/grad_weight/ppermute | solution.py:122
  243.1 94.8 %collective-permute-start.14 = (bf16[384,1024]{1,0:T(8,128)(2,1)}, bf16[384,1024]{1,0:T(8,128)(2,1)}, u32[]{:S(2)}, u32[]{:S(2)}) collective-permute-start(bf16[384,1024]{1,0:T(8,128)(2,1)} %convolution_convert_fusion.10), channel_id=1, source_target_pairs={{0,4},{2,6},{4,0},{6,2},{1,5},{3,7},{5,1},{7,3},{8,12},{10,14},{12... | collective-permute-start | bytes 2359304 | tf_op jit(solution)/shard_map/grad_weight/ppermute | solution.py:122
  256.4 81.6 %collective-permute-start.13 = (bf16[384,1024]{1,0:T(8,128)(2,1)}, bf16[384,1024]{1,0:T(8,128)(2,1)}, u32[]{:S(2)}, u32[]{:S(2)}) collective-permute-start(bf16[384,1024]{1,0:T(8,128)(2,1)} %convolution_convert_fusion.11), channel_id=1, source_target_pairs={{0,6},{2,4},{4,2},{6,0},{1,7},{3,5},{5,3},{7,1},{8,14},{10,12},{12... | collective-permute-start | bytes 2359304 | tf_op jit(solution)/shard_map/grad_weight/ppermute | solution.py:122
  299.7 29.3 %all-to-all-start.2 = ((bf16[16,128,128]{2,1,0:T(8,128)(2,1)}), bf16[16,128,128]{2,1,0:T(8,128)(2,1)}, u32[]{:S(2)}, u32[]{:S(2)}) async-start(bf16[16,128,128]{2,1,0:T(8,128)(2,1)} %copy-done.10), calls=%async_computation.3 | async-start | bytes 1048576 | tf_op jit(solution)/shard_map/back_states/all_to_all | solution.py:179
  318.9 23.2 %collective-permute-start.21 = (bf16[384,1024]{1,0:T(8,128)(2,1)}, bf16[384,1024]{1,0:T(8,128)(2,1)}, u32[]{:S(2)}, u32[]{:S(2)}) collective-permute-start(bf16[384,1024]{1,0:T(8,128)(2,1)} %convolution_convert_fusion.5), channel_id=1, source_target_pairs={{0,2},{2,0},{4,6},{6,4},{1,3},{3,1},{5,7},{7,5},{8,10},{10,8},{12,... | collective-permute-start | bytes 2359304 | tf_op jit(solution)/shard_map/grad_weight/ppermute | solution.py:122
  320.7 25.4 %collective-permute-start.20 = (bf16[384,1024]{1,0:T(8,128)(2,1)}, bf16[384,1024]{1,0:T(8,128)(2,1)}, u32[]{:S(2)}, u32[]{:S(2)}) collective-permute-start(bf16[384,1024]{1,0:T(8,128)(2,1)} %convolution_convert_fusion.6), channel_id=1, source_target_pairs={{0,4},{2,6},{4,0},{6,2},{1,5},{3,7},{5,1},{7,3},{8,12},{10,14},{12... | collective-permute-start | bytes 2359304 | tf_op jit(solution)/shard_map/grad_weight/ppermute | solution.py:122
  325.7 34.9 %collective-permute-start.19 = (bf16[384,1024]{1,0:T(8,128)(2,1)}, bf16[384,1024]{1,0:T(8,128)(2,1)}, u32[]{:S(2)}, u32[]{:S(2)}) collective-permute-start(bf16[384,1024]{1,0:T(8,128)(2,1)} %convolution_convert_fusion.7), channel_id=1, source_target_pairs={{0,6},{2,4},{4,2},{6,0},{1,7},{3,5},{5,3},{7,1},{8,14},{10,12},{12... | collective-permute-start | bytes 2359304 | tf_op jit(solution)/shard_map/grad_weight/ppermute | solution.py:122
  331.0 35.2 %all-to-all-start.3 = ((bf16[16,128,128]{2,1,0:T(8,128)(2,1)}), bf16[16,128,128]{2,1,0:T(8,128)(2,1)}, u32[]{:S(2)}, u32[]{:S(2)}) async-start(bf16[16,128,128]{2,1,0:T(8,128)(2,1)} %back_states.3), calls=%async_computation.4 | async-start | bytes 1048576 | tf_op jit(solution)/shard_map/back_states/all_to_all | solution.py:194
  (33 other events, 551.4 us)
Sparse Core Ops, SparseCore 0:
  132.6 118.0 reduce-scatter.1
